TPU v7x, 128 devices: a whole 4x4x4 slice. The times are simulated.
128 devices in a mesh: leaf: 8 (over x, core), top: 16 (over z, y).
Axes of the slice: x: 4, y: 4, z: 4, core: 2. Of those that a mesh axis runs over, the one named last changes fastest.
Arguments:
- points: float32 [3, 2621440], P(None, ('leaf', 'top')), may hold values from 0 to 2561, as said below
- vectors: float32 [8, 2621440], P(None, ('leaf', 'top')), may hold values from -6 to 6
- near_offset: int32 [5120, 2], P(('leaf', 'top')), may hold values from -2 to 2, as said below
- leaf_basis: float32 [5120, 512, 128], P(('leaf', 'top')), may hold values from -0.25 to 0.25
- leaf_transfer: float32 [5120, 128, 128], P(('leaf', 'top')), may hold values from -0.5 to 0.5
- far_target: int32 [128, 16, 8], P(('leaf', 'top')), may hold values from 0 to 40, as said below
- far_source: int32 [128, 16, 8], P(('leaf', 'top')), may hold values from 0 to 39
- far_coupling: float32 [128, 16, 8, 128, 128], P(('leaf', 'top')), may hold values from -0.5 to 0.5
- upper_transfer: float32 [12, 128, 128], replicated, may hold values from -0.375 to 0.375
- upper_coupling: float32 [14, 128, 128], replicated, may hold values from -0.01953125 to 0.01953125
Outputs:
- product: float32 [8, 2621440], P(None, ('leaf', 'top'))
Inputs may be any that keep to these rules, and one draw needn't show every extreme that they name: Coordinate 0 of the points of leaf g lies in [g / 2, g / 2 + 1], coordinates 1 and 2 in [0, 1]. `near_offset`: 0 marks an empty slot; the nonzero offsets of a leaf are distinct and lead to a leaf of the grid. `far_target`: 40 marks an empty slot; several slots may name the same target.
All inputs are finite; a program needn't handle non-finite values.
Results may differ from a plain program's by a relative error of at most 0.0003.
Values sent between devices are 32-bit elements; how exact they have to be, the bound alone decides.
No kernel may reach another device: no remote copies, remote signals or barrier semaphores. Data moves between devices by JAX's collectives and lax.ppermute only.
A program may use at most 128 MiB of HBM per device.

v0:
```python
import functools
import math

import jax
import jax.numpy as jnp
from jax import lax
from jax.experimental import pallas as pl
from jax.experimental.pallas import tpu as pltpu
from jax.sharding import PartitionSpec as P

F32, BF16 = jnp.float32, jnp.bfloat16
NUGGET = 0.1
SCALES = (0.3, 0.15, 0.15)
LOG2E = math.log2(math.e)
FACTOR = tuple(math.sqrt(3.0) * LOG2E / scale for scale in SCALES)
GAIN = -0.25 * math.log(2.0) * math.e
TINY = 1e-20
DEPTH = 64
HALO = 2
VMEM_LIMIT = 48 << 20
WIDE_LIMIT = 56 << 20


def halves(x):
    high = x.astype(BF16)
    return high, (x - high.astype(F32)).astype(BF16)


def thirds(x):
    high = x.astype(BF16).astype(F32)
    rest = x - high
    middle = rest.astype(BF16).astype(F32)
    return high, middle, rest - middle


def dot_plain(x, matrix):
    n = matrix.shape[1]
    left = jnp.concatenate(halves(x), axis=0)
    out = jnp.dot(left, jnp.concatenate(halves(matrix), axis=1), preferred_element_type=F32)
    return out[0:8, 0:n] + out[8:16, 0:n] + out[0:8, n : 2 * n]


def dot_turned(x, matrix):
    high, low = halves(x)
    upper = jnp.concatenate([high, high], axis=1)
    lower = jnp.concatenate([low, jnp.zeros_like(low)], axis=1)
    out = lax.dot_general(
        jnp.concatenate([upper, lower], axis=0),
        jnp.concatenate(halves(matrix), axis=1),
        (((1,), (1,)), ((), ())),
        preferred_element_type=F32,
    )
    return out[0:8] + out[8:16]


def coef_kernel(place_ref, vec_ref, basis_ref, transfer_ref, up0_ref, up1_ref, coef_ref, part_ref, *, per_step, leaf_size):
    del place_ref
    step = pl.program_id(0)

    @pl.when(step == 0)
    def _():
        part_ref[...] = jnp.zeros_like(part_ref)

    total = jnp.zeros(part_ref.shape[1:], F32)
    for i in range(per_step):
        coef = dot_plain(vec_ref[:, i * leaf_size : (i + 1) * leaf_size], basis_ref[i])
        coef_ref[i] = coef
        total += dot_plain(coef, transfer_ref[i])
    part_ref[0] += total

    @pl.when(step == pl.num_programs(0) - 1)
    def _():
        part_ref[1] = dot_plain(part_ref[0], up0_ref[0])
        part_ref[2] = dot_plain(part_ref[1], up1_ref[0])


def coefficients(place, vectors, leaf_basis, leaf_transfer, upper_transfer):
    leaves, leaf_size, rank = leaf_basis.shape
    columns = vectors.shape[0]
    per_step = 5
    node = (1, rank, rank)
    return pl.pallas_call(
        functools.partial(coef_kernel, per_step=per_step, leaf_size=leaf_size),
        grid_spec=pltpu.PrefetchScalarGridSpec(
            num_scalar_prefetch=1,
            grid=(leaves // per_step,),
            in_specs=[
                pl.BlockSpec((columns, per_step * leaf_size), lambda i, p: (0, i)),
                pl.BlockSpec((per_step, leaf_size, rank), lambda i, p: (i, 0, 0)),
                pl.BlockSpec((per_step, rank, rank), lambda i, p: (i, 0, 0)),
                pl.BlockSpec(node, lambda i, p: (p[0], 0, 0)),
                pl.BlockSpec(node, lambda i, p: (8 + (p[0] >> 1), 0, 0)),
            ],
            out_specs=[
                pl.BlockSpec((per_step, columns, rank), lambda i, p: (i, 0, 0)),
                pl.BlockSpec((3, columns, rank), lambda i, p: (0, 0, 0)),
            ],
        ),
        out_shape=[
            jax.ShapeDtypeStruct((leaves, columns, rank), F32),
            jax.ShapeDtypeStruct((3, columns, rank), F32),
        ],
        compiler_params=pltpu.CompilerParams(vmem_limit_bytes=WIDE_LIMIT),
        cost_estimate=pl.CostEstimate(
            flops=leaves * 16 * rank * (leaf_size + rank) * 4,
            bytes_accessed=4 * leaves * rank * (leaf_size + rank),
            transcendentals=0,
        ),
    )(place, vectors, leaf_basis, leaf_transfer, upper_transfer, upper_transfer)


def features(x, target):
    row = lax.broadcasted_iota(jnp.int32, x.shape, 0)
    norm = jnp.sum(x * x, axis=0, keepdims=True)
    high, middle, low = thirds(jnp.where(row < 3, x, norm))
    norm_row, one_row, factor = (4, 3, -2.0) if target else (3, 4, 1.0)

    def group(coordinates, norms):
        out = jnp.where(row < 3, coordinates * factor, 0.0)
        if norms is not None:
            out = jnp.where(row == norm_row, norms, jnp.where(row == one_row, 1.0, out))
        return out

    if target:
        groups = [group(high, high), group(middle, middle), group(high, low)]
        groups += [group(low, None), group(middle, None), group(high, None)]
    else:
        groups = [group(high, high), group(middle, middle), group(low, low)]
        groups += [group(high, None), group(high, None), group(middle, None)]
    groups += [jnp.zeros_like(x)] * (DEPTH // 8 - 6)
    return jnp.concatenate(groups, axis=0)


def matern(dist_sq):
    dist_sq = jnp.maximum(dist_sq, TINY)
    nt = -LOG2E - dist_sq * lax.rsqrt(dist_sq)
    return nt * jnp.exp2(nt)


def near_kernel(
    first_ref,
    offset_ref,
    points_ref,
    vectors_ref,
    before_p,
    before_v,
    after_p,
    after_v,
    out_ref,
    wide_scr,
    x_scr,
    a_scr,
    v_scr,
    b0,
    b1,
    u0,
    u1,
    kh0,
    kh1,
    kl0,
    kl1,
    item_g,
    item_h,
    *,
    lo,
    hi,
    leaf_size,
):
    rows = leaf_size // 2
    leaves = offset_ref.shape[0]
    first = first_ref[0]
    row8 = lax.broadcasted_iota(jnp.int32, (8, leaf_size), 0)

    def clear(ref):
        def turn(i, _):
            ref[pl.ds(pl.multiple_of(i * 16, 16), 16)] = jnp.zeros((16, leaf_size), ref.dtype)
            return 0

        lax.fori_loop(0, leaf_size // 16, turn, 0)

    for ref in (u0, u1, kh0, kh1, kl0, kl1):
        clear(ref)
    wide_scr[...] = jnp.zeros_like(wide_scr)

    def prepare(p_ref, v_ref, start, stop, origin):
        def turn(h, _):
            at = pl.ds(pl.multiple_of((h - origin) * leaf_size, leaf_size), leaf_size)
            to = h + HALO - lo
            centre = (first + h).astype(F32) * 0.5 + 0.5
            wide_scr[0:3] = p_ref[:, at]
            shift = jnp.where(row8 == 0, centre, 0.5)
            scale = jnp.where(row8 == 0, FACTOR[0], FACTOR[1])
            x = jnp.where(row8 < 3, (wide_scr[...] - shift) * scale, 0.0)
            x_scr[to] = x
            a_scr[to] = features(x, False).T.astype(BF16)
            v_high, v_low = halves(v_ref[:, at])
            v_scr[to, 0:16] = jnp.concatenate([v_high, v_low], axis=0)
            v_scr[to, 16:32] = jnp.concatenate([v_high, jnp.zeros_like(v_high)], axis=0)
            return 0

        lax.fori_loop(start, stop, turn, 0)

    if lo < HALO:
        prepare(before_p, before_v, -HALO, 0, -HALO)
    prepare(points_ref, vectors_ref, max(lo - HALO, 0), min(hi + HALO, leaves), 0)
    if hi > leaves - HALO:
        prepare(after_p, after_v, leaves, leaves + HALO, leaves)

    def listing(g, n):
        at = pl.ds(pl.multiple_of(g * leaf_size, leaf_size), leaf_size)
        to = pl.ds(pl.multiple_of((g - lo) * leaf_size, leaf_size), leaf_size)
        out_ref[:, to] = NUGGET * vectors_ref[:, at]
        item_g[n] = g - lo
        item_h[n] = g - lo + HALO
        n = n + 1
        for j in range(offset_ref.shape[1]):
            offset = offset_ref[g, j]
            item_g[n] = g - lo
            item_h[n] = g - lo + HALO + offset
            n = n + jnp.where(offset != 0, 1, 0)
        return n

    count = lax.fori_loop(lo, hi, listing, 0)

    def target_features(i, b_scr):
        i = jnp.minimum(i, count - 1)
        g, h = item_g[i], item_h[i]
        apart = (g + HALO - h).astype(F32) * (0.5 * FACTOR[0])
        x = x_scr[g + HALO]
        b_scr[...] = features(jnp.where(row8 == 0, x + apart, x), True).astype(BF16)

    def turn(i, b_now, b_next, u_write, u_read, kh_write, kl_write, kh_read, kl_read):
        h_now = item_h[jnp.minimum(i, count - 1)]
        old = jnp.clip(i - 2, 0, count - 1)
        h_old = item_h[old]
        acc = jnp.zeros((16, leaf_size), F32)
        for c in range(0, leaf_size, rows):
            u_write[c : c + rows] = jnp.dot(a_scr[h_now, c : c + rows], b_now[...], preferred_element_type=F32)
            for r in range(c, c + rows, 16):
                high, low = halves(matern(u_read[r : r + 16]))
                kh_write[r : r + 16] = high
                kl_write[r : r + 16] = low
            acc += jnp.dot(v_scr[h_old, 0:16, c : c + rows], kh_read[c : c + rows], preferred_element_type=F32)
            acc += jnp.dot(v_scr[h_old, 16:32, c : c + rows], kl_read[c : c + rows], preferred_element_type=F32)
        target_features(i + 1, b_next)
        done = (acc[0:8] + acc[8:16]) * jnp.where((i >= 2) & (i < count + 2), GAIN, 0.0)
        at = pl.ds(pl.multiple_of(item_g[old] * leaf_size, leaf_size), leaf_size)
        out_ref[:, at] += done

    target_features(0, b0)

    def two_turns(i, _):
        turn(2 * i, b0, b1, u0, u1, kh0, kl0, kh1, kl1)
        turn(2 * i + 1, b1, b0, u1, u0, kh1, kl1, kh0, kl0)
        return 0

    lax.fori_loop(0, (count + 3) >> 1, two_turns, 0)


def near_field(first, near_offset, points, vectors, before, after, lo, hi):
    leaves, slots = near_offset.shape
    columns = vectors.shape[0]
    leaf_size = vectors.shape[1] // leaves
    count = hi - lo
    smem, vmem = pl.BlockSpec(memory_space=pltpu.SMEM), pl.BlockSpec(memory_space=pltpu.VMEM)
    square = (leaf_size, leaf_size)
    return pl.pallas_call(
        functools.partial(near_kernel, lo=lo, hi=hi, leaf_size=leaf_size),
        in_specs=[smem, smem] + [vmem] * 6,
        out_specs=vmem,
        out_shape=jax.ShapeDtypeStruct((columns, count * leaf_size), F32),
        scratch_shapes=[
            pltpu.VMEM((8, leaf_size), F32),
            pltpu.VMEM((count + 2 * HALO, 8, leaf_size), F32),
            pltpu.VMEM((count + 2 * HALO, leaf_size, DEPTH), BF16),
            pltpu.VMEM((count + 2 * HALO, 32, leaf_size), BF16),
            pltpu.VMEM((DEPTH, leaf_size), BF16),
            pltpu.VMEM((DEPTH, leaf_size), BF16),
            pltpu.VMEM(square, F32),
            pltpu.VMEM(square, F32),
            pltpu.VMEM(square, BF16),
            pltpu.VMEM(square, BF16),
            pltpu.VMEM(square, BF16),
            pltpu.VMEM(square, BF16),
            pltpu.SMEM((count * (slots + 1) + 8,), jnp.int32),
            pltpu.SMEM((count * (slots + 1) + 8,), jnp.int32),
        ],
        compiler_params=pltpu.CompilerParams(vmem_limit_bytes=VMEM_LIMIT),
        cost_estimate=pl.CostEstimate(
            flops=count * 3 * leaf_size * leaf_size * 512,
            bytes_accessed=8 * 11 * leaves * leaf_size,
            transcendentals=count * 6 * leaf_size * leaf_size,
        ),
    )(first, near_offset, points, vectors, before[0], before[1], after[0], after[1])


def far_kernel(
    place_ref,
    target_ref,
    source_ref,
    parts_ref,
    down0_ref,
    down1_ref,
    across0_ref,
    across1_ref,
    across2_ref,
    coef_ref,
    coupling_ref,
    transfer_ref,
    basis_ref,
    near_ref,
    out_ref,
    local_scr,
    region_scr,
    *,
    far_steps,
    peers,
    per_step,
):
    step = pl.program_id(0)
    leaf_size = basis_ref.shape[1]
    per_far, slots = coupling_ref.shape[0], coupling_ref.shape[1]

    @pl.when(step == 0)
    def _():
        local_scr[...] = jnp.zeros_like(local_scr)
        here = place_ref[0]

        def summed(level):
            first = ((here >> level) ^ 1) << level
            chains = [None] * 4
            for i in range(peers << level):
                part = parts_ref[3 * (first * peers + i) + level]
                chains[i % 4] = part if chains[i % 4] is None else chains[i % 4] + part
            return (chains[0] + chains[1]) + (chains[2] + chains[3])

        local = dot_plain(summed(2), across2_ref[0])
        local = dot_plain(summed(1), across1_ref[0]) + dot_turned(local, down1_ref[0])
        region_scr[...] = dot_plain(summed(0), across0_ref[0]) + dot_turned(local, down0_ref[0])

    @pl.when(step < far_steps)
    def _():
        for p in range(per_far):
            for k in range(slots):
                coef = coef_ref[p, source_ref[step * per_far + p, k]]
                local_scr[target_ref[step * per_far + p, k]] += dot_plain(coef, coupling_ref[p, k])

    @pl.when(step >= far_steps)
    def _():
        for i in range(per_step):
            local = local_scr[(step - far_steps) * per_step + i] + dot_turned(region_scr[...], transfer_ref[i])
            at = slice(i * leaf_size, (i + 1) * leaf_size)
            out_ref[:, at] = near_ref[:, at] + dot_turned(local, basis_ref[i])


def far_field(place, targets, sources, parts, coefs, far_coupling, upper_transfer, upper_coupling, leaf_transfer, leaf_basis, near):
    peers, slots = sources.shape
    leaves, leaf_size, rank = leaf_basis.shape
    columns = near.shape[0]
    per_step, per_far = 5, 2
    far_steps = peers // per_far
    node = (1, rank, rank)

    def soon(i):
        return jnp.minimum(i, far_steps - 1)

    def late(i):
        return jnp.maximum(i - far_steps, 0)

    return pl.pallas_call(
        functools.partial(far_kernel, far_steps=far_steps, peers=peers, per_step=per_step),
        grid_spec=pltpu.PrefetchScalarGridSpec(
            num_scalar_prefetch=3,
            grid=(far_steps + leaves // per_step,),
            in_specs=[
                pl.BlockSpec(parts.shape, lambda i, p, t, s: (0, 0, 0)),
                pl.BlockSpec(node, lambda i, p, t, s: (p[0], 0, 0)),
                pl.BlockSpec(node, lambda i, p, t, s: (8 + (p[0] >> 1), 0, 0)),
                pl.BlockSpec(node, lambda i, p, t, s: (p[0], 0, 0)),
                pl.BlockSpec(node, lambda i, p, t, s: (8 + (p[0] >> 1), 0, 0)),
                pl.BlockSpec(node, lambda i, p, t, s: (12 + (p[0] >> 2), 0, 0)),
                pl.BlockSpec((per_far, leaves, columns, rank), lambda i, p, t, s: (soon(i), 0, 0, 0)),
                pl.BlockSpec((per_far, slots, rank, rank), lambda i, p, t, s: (soon(i), 0, 0, 0)),
                pl.BlockSpec((per_step, rank, rank), lambda i, p, t, s: (late(i), 0, 0)),
                pl.BlockSpec((per_step, leaf_size, rank), lambda i, p, t, s: (late(i), 0, 0)),
                pl.BlockSpec((columns, per_step * leaf_size), lambda i, p, t, s: (0, late(i))),
            ],
            out_specs=pl.BlockSpec((columns, per_step * leaf_size), lambda i, p, t, s: (0, late(i))),
            scratch_shapes=[pltpu.VMEM((leaves + 1, columns, rank), F32), pltpu.VMEM((columns, rank), F32)],
        ),
        out_shape=jax.ShapeDtypeStruct(near.shape, F32),
        compiler_params=pltpu.CompilerParams(vmem_limit_bytes=WIDE_LIMIT),
    )(
        place,
        targets,
        sources,
        parts,
        upper_transfer,
        upper_transfer,
        upper_coupling,
        upper_coupling,
        upper_coupling,
        coefs,
        far_coupling,
        leaf_transfer,
        leaf_basis,
        near,
    )


def neighbours(points, vectors, width):
    axes = ("leaf", "top")
    count = lax.axis_size("leaf") * lax.axis_size("top")
    joined = [jnp.concatenate([points[:, s], vectors[:, s]], axis=0) for s in (slice(-width, None), slice(0, width))]
    before = lax.ppermute(joined[0], axes, [(i, i + 1) for i in range(count - 1)])
    after = lax.ppermute(joined[1], axes, [(i + 1, i) for i in range(count - 1)])
    return (before[:3], before[3:]), (after[:3], after[3:])


def shards(
    points,
    vectors,
    near_offset,
    leaf_basis,
    leaf_transfer,
    far_target,
    far_source,
    far_coupling,
    upper_transfer,
    upper_coupling,
):
    leaves, leaf_size, _ = leaf_basis.shape
    peers = lax.axis_size("top")
    region, peer = lax.axis_index("leaf"), lax.axis_index("top")
    place = region.astype(jnp.int32).reshape(1)
    first = ((region * peers + peer) * leaves).astype(jnp.int32).reshape(1)

    before, after = neighbours(points, vectors, HALO * leaf_size)
    coefs, parts = coefficients(place, vectors, leaf_basis, leaf_transfer, upper_transfer)
    all_parts = lax.all_gather(parts, ("leaf", "top"), axis=0, tiled=True)
    all_coefs = lax.all_gather(coefs, "top", axis=0)
    near = near_field(first, near_offset, points, vectors, before, after, 0, leaves)
    return far_field(
        place,
        far_target[0],
        far_source[0],
        all_parts,
        all_coefs,
        far_coupling[0],
        upper_transfer,
        upper_coupling,
        leaf_transfer,
        leaf_basis,
        near,
    )


def solution(mesh):
    split = ("leaf", "top")
    in_specs = (
        P(None, split),
        P(None, split),
        P(split, None),
        P(split, None, None),
        P(split, None, None),
        P(split, None, None),
        P(split, None, None),
        P(split, None, None, None, None),
        P(),
        P(),
    )
    return jax.shard_map(shards, mesh=mesh, in_specs=in_specs, out_specs=P(None, split), check_vma=False)
```

profile of v0, /device:TPU:2, one launch (start us, length us, event | category | flops | bytes accessed | tf_op | source)
XLA Modules:
  0.0 157.9 jit_solution(781698467841644396)
XLA Ops:
  6.5 0.0 all-gather.4.cloned.1.call-start
  6.5 0.0 copy-start.2
  6.5 0.0 copy-start
  6.5 0.0 copy-start.3
  6.5 0.0 copy-start.4
  6.5 0.0 copy-start.5
  6.6 11.8 %shard_map.100 = (f32[40,8,128]{2,1,0:T(8,128)}, f32[3,8,128]{2,1,0:T(8,128)}) custom-call(s32[1]{0:T(128)} %bitcast.place_ref, f32[8,20480]{1,0:T(8,128)} %vectors_ref.1, f32[40,512,128]{2,1,0:T(8,128)} %basis_ref.3, f32[40,128,128]{2,1,0:T(8,128)} %transfer_ref.3, f32[12,128,128]{2,1,0:T(8,128)} %down1_ref.1, f32[12,128,128]{2,1,0:T(8,128)} %down1_ref.1), custom_call_target="tpu_custom_call" | custom-call | flops 209715200 | bytes 13107200 | tf_op jit(solution)/shard_map/pallas_call | solution.py:82
  18.4 0.0 all-gather.4.cloned.1.call-update
  18.4 0.0 all-gather.6.cloned.1.call-start
  18.5 0.7 all-gather.6.cloned.1.call-update
  19.2 0.0 copy-done.2
  19.2 0.0 copy-done
  19.2 3.5 %collective-permute-start = (f32[11,1024]{1,0:T(8,128)S(1)}, f32[11,1024]{1,0:T(8,128)S(1)}, u32[]{:S(2)}, u32[]{:S(2)}) collective-permute-start(f32[11,1024]{1,0:T(8,128)S(1)} %pad_maximum_fusion), channel_id=1, source_target_pairs={{0,1},{1,2},{2,3},{3,4},{4,5},{5,6},{6,7},{7,8},{8,9},{9,10},{10,1... | collective-permute-start | bytes 135176 | tf_op jit(solution)/shard_map/ppermute | solution.py:415
  22.7 6.3 %collective-permute-start.1 = (f32[11,1024]{1,0:T(8,128)S(1)}, f32[11,1024]{1,0:T(8,128)S(1)}, u32[]{:S(2)}, u32[]{:S(2)}) collective-permute-start(f32[11,1024]{1,0:T(8,128)S(1)} %pad_maximum_fusion.1), channel_id=1, source_target_pairs={{1,0},{2,1},{3,2},{4,3},{5,4},{6,5},{7,6},{8,7},{9,8},{10,9},{11,1... | collective-permute-start | bytes 135176 | tf_op jit(solution)/shard_map/ppermute | solution.py:416
  29.0 0.0 copy-done.3
  29.1 0.7 copy.15.target_ref
  29.7 0.0 copy-done.4
  29.7 0.7 copy.16.source_ref
  30.4 0.0 copy-done.5
  30.4 0.1 copy.14.offset_ref
  30.5 0.0 collective-permute-done
  30.5 0.4 collective-permute-done.1
  30.9 67.3 %shard_map.101.near_ref = f32[8,20480]{1,0:T(8,128)S(1)} custom-call(s32[1]{0:T(128)} %bitcast.5.first_ref, s32[40,2]{1,0:T(8,128)S(1)} %copy.14.offset_ref, f32[3,20480]{1,0:T(4,128)S(1)} %copy-done.2, f32[8,20480]{1,0:T(8,128)S(1)} %copy-done, f32[3,1024]{1,0:T(4,128)S(1)} %slice.32.before_p, f32[8,1024]{1,0:T(8,128)S(1)} %slice.33.before_v, ...), custom_call_target="tpu_custom_call" | custom-call | flops 16106127360 | bytes 1802240 | tf_op jit(solution)/shard_map/pallas_call | solution.py:267
  98.3 0.0 copy-start.1
  98.3 0.8 copy-done.1
  99.1 0.0 all-gather.4.cloned.1.call-done.parts_ref
  99.1 32.1 %all-gather.6.cloned.1.call-done = f32[640,8,128]{2,1,0:T(8,128)} async-done(((f32[40,8,128]{2,1,0:T(8,128)}), f32[640,8,128]{2,1,0:T(8,128)}) %all-gather.6.cloned.1.call-update) | async-done | bytes 2621456 | tf_op jit(solution)/shard_map/all_gather | solution.py:441
  131.2 19.9 %shard_map.102 = f32[8,20480]{1,0:T(8,128)} custom-call(s32[1]{0:T(128)} %bitcast.place_ref, s32[16,8]{1,0:T(8,128)} %copy.15.target_ref, s32[16,8]{1,0:T(8,128)} %copy.16.source_ref, f32[384,8,128]{2,1,0:T(8,128)} %all-gather.4.cloned.1.call-done.parts_ref, f32[12,128,128]{2,1,0:T(8,128)} %down1_ref.1, f32[12,128,128]{2,1,0:T(8,128)} %down1_ref.1, ...), custom_call_target="tpu_custom_call" | custom-call | tf_op jit(solution)/shard_map/pallas_call | solution.py:370
  (8 shorter events, 0.1 us)
Async XLA Ops:
  6.5 92.6 %all-gather.4.cloned.1.call-start = ((), (), s32[]{:S(2)}) async-start(), calls=%async_computation | async-start | bytes 1585152 | tf_op jit(solution)/shard_map/all_gather | solution.py:440
  6.5 12.6 %copy-start.2 = (f32[3,20480]{1,0:T(4,128)S(1)}, f32[3,20480]{1,0:T(4,128)}, u32[]{:S(2)}) copy-start(f32[3,20480]{1,0:T(4,128)} %points_ref.1) | copy-start | bytes 737284
  6.5 12.6 %copy-start = (f32[8,20480]{1,0:T(8,128)S(1)}, f32[8,20480]{1,0:T(8,128)}, u32[]{:S(2)}) copy-start(f32[8,20480]{1,0:T(8,128)} %vectors_ref.1) | copy-start | bytes 1966084
  6.5 22.5 %copy-start.3 = (s32[1,16,8]{1,2,0:T(8,128)S(1)}, s32[1,16,8]{1,2,0:T(8,128)}, u32[]{:S(2)}) copy-start(s32[1,16,8]{1,2,0:T(8,128)} %param.15) | copy-start | bytes 1540
  6.5 23.2 %copy-start.4 = (s32[1,16,8]{1,2,0:T(8,128)S(1)}, s32[1,16,8]{1,2,0:T(8,128)}, u32[]{:S(2)}) copy-start(s32[1,16,8]{1,2,0:T(8,128)} %param.16) | copy-start | bytes 1540
  6.5 23.8 %copy-start.5 = (s32[40,2]{0,1:T(2,128)S(1)}, s32[40,2]{0,1:T(2,128)}, u32[]{:S(2)}) copy-start(s32[40,2]{0,1:T(2,128)} %param.12) | copy-start | bytes 964
  18.4 112.8 %all-gather.6.cloned.1.call-start = ((), (), s32[]{:S(2)}) async-start(), calls=%async_computation.1 | async-start | bytes 2785280 | tf_op jit(solution)/shard_map/all_gather | solution.py:441
  19.2 11.3 %collective-permute-start = (f32[11,1024]{1,0:T(8,128)S(1)}, f32[11,1024]{1,0:T(8,128)S(1)}, u32[]{:S(2)}, u32[]{:S(2)}) collective-permute-start(f32[11,1024]{1,0:T(8,128)S(1)} %pad_maximum_fusion), channel_id=1, source_target_pairs={{0,1},{1,2},{2,3},{3,4},{4,5},{5,6},{6,7},{7,8},{8,9},{9,10},{10,1... | collective-permute-start | bytes 135176 | tf_op jit(solution)/shard_map/ppermute | solution.py:415
  22.7 8.2 %collective-permute-start.1 = (f32[11,1024]{1,0:T(8,128)S(1)}, f32[11,1024]{1,0:T(8,128)S(1)}, u32[]{:S(2)}, u32[]{:S(2)}) collective-permute-start(f32[11,1024]{1,0:T(8,128)S(1)} %pad_maximum_fusion.1), channel_id=1, source_target_pairs={{1,0},{2,1},{3,2},{4,3},{5,4},{6,5},{7,6},{8,7},{9,8},{10,9},{11,1... | collective-permute-start | bytes 135176 | tf_op jit(solution)/shard_map/ppermute | solution.py:416
  98.3 0.8 copy-start.1
Sparse Core Ops, SparseCore 0:
  18.5 65.3 all-gather.3
  86.1 45.0 all-gather.5
where the time goes:
time: 159 us; the launch traced here: 158 us
  Pallas kernels  99.1 us (62%)
  waiting for transfers between devices  33.2 us (21%)
  between operations  13.5 us (8%)
  starting transfers between devices  9.82 us (6%)
  local copies, waits for them, and re-layouts  2.32 us (1%)
    pallas_call x1, Pallas kernels, near_field(): pl.pallas_call(functools.partial(near_kernel, lo=lo, hi=hi, leaf_size=lea...  67.3 us
    all_gather x1, waiting for transfers between devices, shards(): all_coefs = lax.all_gather(coefs, 'top', axis=0)  32.1 us
    pallas_call x1, Pallas kernels, far_field(): pl.pallas_call(functools.partial(far_kernel, far_steps=far_steps, peers=p...  19.9 us
    pallas_call x1, Pallas kernels, coefficients(): pl.pallas_call(functools.partial(coef_kernel, per_step=per_step, leaf_siz...  11.8 us
    ppermute x1, starting transfers between devices, neighbours(): lax.ppermute(joined[1], axes, [(i + 1, i) for i in range(count - 1)])  6.3 us
    ppermute x1, starting transfers between devices, neighbours(): lax.ppermute(joined[0], axes, [(i, i + 1) for i in range(count - 1)])  3.48 us
  transfers between devices with their start and end apart: 4, of which 2 were waited for; matrix products, arithmetic and copies ran while one was open for 1% of the time, Pallas kernels for 43%

commit v1 on v0

v1 whole, which is shorter than its diff:
```python
import functools
import math

import jax
import jax.numpy as jnp
from jax import lax
from jax.experimental import pallas as pl
from jax.experimental.pallas import tpu as pltpu
from jax.sharding import PartitionSpec as P

F32, BF16 = jnp.float32, jnp.bfloat16
NUGGET = 0.1
SCALES = (0.3, 0.15, 0.15)
LOG2E = math.log2(math.e)
FACTOR = tuple(math.sqrt(3.0) * LOG2E / scale for scale in SCALES)
GAIN = -0.25 * math.log(2.0) * math.e
TINY = 1e-20
DEPTH = 64
HALO = 2
NEAR_LIMIT = 20 << 20
WIDE_LIMIT = 56 << 20
EARLY_LEAVES = 26


def halves(x):
    high = x.astype(BF16)
    return high, (x - high.astype(F32)).astype(BF16)


def thirds(x):
    high = x.astype(BF16).astype(F32)
    rest = x - high
    middle = rest.astype(BF16).astype(F32)
    return high, middle, rest - middle


def dot_plain(x, matrix):
    n = matrix.shape[1]
    left = jnp.concatenate(halves(x), axis=0)
    out = jnp.dot(left, jnp.concatenate(halves(matrix), axis=1), preferred_element_type=F32)
    return out[0:8, 0:n] + out[8:16, 0:n] + out[0:8, n : 2 * n]


def dot_turned(x, matrix):
    high, low = halves(x)
    upper = jnp.concatenate([high, high], axis=1)
    lower = jnp.concatenate([low, jnp.zeros_like(low)], axis=1)
    out = lax.dot_general(
        jnp.concatenate([upper, lower], axis=0),
        jnp.concatenate(halves(matrix), axis=1),
        (((1,), (1,)), ((), ())),
        preferred_element_type=F32,
    )
    return out[0:8] + out[8:16]


def coef_kernel(place_ref, vec_hbm, basis_hbm, transfer_hbm, up0_ref, up1_ref, coef_ref, part_ref, vec, basis, transfer, sems, *, group):
    del place_ref
    leaves, leaf_size, _ = basis.shape
    groups = leaves // group

    def copies(i):
        at = pl.ds(i * group, group)
        points = pl.ds(pl.multiple_of(i * (group * leaf_size), group * leaf_size), group * leaf_size)
        return (
            pltpu.make_async_copy(vec_hbm.at[:, points], vec.at[:, points], sems.at[0, i]),
            pltpu.make_async_copy(basis_hbm.at[at], basis.at[at], sems.at[1, i]),
            pltpu.make_async_copy(transfer_hbm.at[at], transfer.at[at], sems.at[2, i]),
        )

    for i in range(groups):
        for copy in copies(i):
            copy.start()

    def turn(i, total):
        for copy in copies(i):
            copy.wait()
        coefs = []
        for j in range(group):
            at = pl.ds(pl.multiple_of((i * group + j) * leaf_size, leaf_size), leaf_size)
            coefs.append(dot_plain(vec[:, at], basis[i * group + j]))
        for j in range(group):
            coef_ref[i * group + j] = coefs[j]
            total += dot_plain(coefs[j], transfer[i * group + j])
        return total

    part = lax.fori_loop(0, groups, turn, jnp.zeros(part_ref.shape[1:], F32))
    part_ref[0] = part
    part = dot_plain(part, up0_ref[0])
    part_ref[1] = part
    part_ref[2] = dot_plain(part, up1_ref[0])


def coefficients(place, vectors, leaf_basis, leaf_transfer, upper_transfer):
    leaves, leaf_size, rank = leaf_basis.shape
    columns = vectors.shape[0]
    group = 4
    node = (1, rank, rank)
    hbm = pl.BlockSpec(memory_space=pl.ANY)
    return pl.pallas_call(
        functools.partial(coef_kernel, group=group),
        grid_spec=pltpu.PrefetchScalarGridSpec(
            num_scalar_prefetch=1,
            grid=(1,),
            in_specs=[
                hbm,
                hbm,
                hbm,
                pl.BlockSpec(node, lambda i, p: (p[0], 0, 0)),
                pl.BlockSpec(node, lambda i, p: (8 + (p[0] >> 1), 0, 0)),
            ],
            out_specs=[
                pl.BlockSpec((leaves + 3, columns, rank), lambda i, p: (0, 0, 0)),
                pl.BlockSpec((3, columns, rank), lambda i, p: (0, 0, 0)),
            ],
            scratch_shapes=[
                pltpu.VMEM(vectors.shape, F32),
                pltpu.VMEM(leaf_basis.shape, F32),
                pltpu.VMEM(leaf_transfer.shape, F32),
                pltpu.SemaphoreType.DMA((3, leaves // group)),
            ],
        ),
        out_shape=[
            jax.ShapeDtypeStruct((leaves + 3, columns, rank), F32),
            jax.ShapeDtypeStruct((3, columns, rank), F32),
        ],
        compiler_params=pltpu.CompilerParams(vmem_limit_bytes=WIDE_LIMIT),
        cost_estimate=pl.CostEstimate(
            flops=leaves * 16 * rank * (leaf_size + rank) * 4,
            bytes_accessed=4 * leaves * rank * (leaf_size + rank),
            transcendentals=0,
        ),
    )(place, vectors, leaf_basis, leaf_transfer, upper_transfer, upper_transfer)


def siblings(parts):
    count = lax.axis_size("leaf")

    def from_partner(x, distance):
        return lax.ppermute(x, "leaf", [(i, i ^ distance) for i in range(count)])

    other = from_partner(parts, 1)
    level0, parts = other[0:1], parts[1:] + other[1:]
    other = from_partner(parts, 2)
    level1, parts = other[0:1], parts[1:] + other[1:]
    return level0, level1, from_partner(parts, 4)


def features(x, target):
    row = lax.broadcasted_iota(jnp.int32, x.shape, 0)
    norm = jnp.sum(x * x, axis=0, keepdims=True)
    high, middle, low = thirds(jnp.where(row < 3, x, norm))
    norm_row, one_row, factor = (4, 3, -2.0) if target else (3, 4, 1.0)

    def group(coordinates, norms):
        out = jnp.where(row < 3, coordinates * factor, 0.0)
        if norms is not None:
            out = jnp.where(row == norm_row, norms, jnp.where(row == one_row, 1.0, out))
        return out

    if target:
        groups = [group(high, high), group(middle, middle), group(high, low)]
        groups += [group(low, None), group(middle, None), group(high, None)]
    else:
        groups = [group(high, high), group(middle, middle), group(low, low)]
        groups += [group(high, None), group(high, None), group(middle, None)]
    groups += [jnp.zeros_like(x)] * (DEPTH // 8 - 6)
    return jnp.concatenate(groups, axis=0)


def matern(dist_sq):
    dist_sq = jnp.maximum(dist_sq, TINY)
    nt = -LOG2E - dist_sq * lax.rsqrt(dist_sq)
    return nt * jnp.exp2(nt)


def near_core(inputs, out_ref, scratch, *, lo, hi, base, leaf_size):
    first_ref, offset_ref, points_ref, vectors_ref, before_p, before_v, after_p, after_v = inputs
    wide_scr, x_scr, a_scr, v_scr, b0, b1, u0, u1, kh0, kh1, kl0, kl1, item_g, item_h = scratch
    rows = leaf_size // 2
    leaves = offset_ref.shape[0]
    first = first_ref[0]
    row8 = lax.broadcasted_iota(jnp.int32, (8, leaf_size), 0)

    def clear(ref):
        def turn(i, _):
            ref[pl.ds(pl.multiple_of(i * 16, 16), 16)] = jnp.zeros((16, leaf_size), ref.dtype)
            return 0

        lax.fori_loop(0, leaf_size // 16, turn, 0)

    for ref in (u0, u1, kh0, kh1, kl0, kl1):
        clear(ref)
    wide_scr[...] = jnp.zeros_like(wide_scr)

    def prepare(p_ref, v_ref, start, stop, origin):
        def turn(h, _):
            at = pl.ds(pl.multiple_of((h - origin) * leaf_size, leaf_size), leaf_size)
            to = h + HALO - lo
            centre = (first + h).astype(F32) * 0.5 + 0.5
            wide_scr[0:3] = p_ref[:, at]
            shift = jnp.where(row8 == 0, centre, 0.5)
            scale = jnp.where(row8 == 0, FACTOR[0], FACTOR[1])
            x = jnp.where(row8 < 3, (wide_scr[...] - shift) * scale, 0.0)
            x_scr[to] = x
            a_scr[to] = features(x, False).T.astype(BF16)
            v_high, v_low = halves(v_ref[:, at])
            v_scr[to, 0:16] = jnp.concatenate([v_high, v_low], axis=0)
            v_scr[to, 16:32] = jnp.concatenate([v_high, jnp.zeros_like(v_high)], axis=0)
            return 0

        lax.fori_loop(start, stop, turn, 0)

    if lo < HALO:
        prepare(before_p, before_v, -HALO, 0, -HALO)
    prepare(points_ref, vectors_ref, max(lo - HALO, 0), min(hi + HALO, leaves), 0)
    if hi > leaves - HALO:
        prepare(after_p, after_v, leaves, leaves + HALO, leaves)

    def listing(g, n):
        at = pl.ds(pl.multiple_of(g * leaf_size, leaf_size), leaf_size)
        to = pl.ds(pl.multiple_of((g - base) * leaf_size, leaf_size), leaf_size)
        out_ref[:, to] = NUGGET * vectors_ref[:, at]
        item_g[n] = g - lo
        item_h[n] = g - lo + HALO
        n = n + 1
        for j in range(offset_ref.shape[1]):
            offset = offset_ref[g, j]
            item_g[n] = g - lo
            item_h[n] = g - lo + HALO + offset
            n = n + jnp.where(offset != 0, 1, 0)
        return n

    count = lax.fori_loop(lo, hi, listing, 0)

    def target_features(i, b_scr):
        i = jnp.minimum(i, count - 1)
        g, h = item_g[i], item_h[i]
        apart = (g + HALO - h).astype(F32) * (0.5 * FACTOR[0])
        x = x_scr[g + HALO]
        b_scr[...] = features(jnp.where(row8 == 0, x + apart, x), True).astype(BF16)

    def turn(i, b_now, b_next, u_write, u_read, kh_write, kl_write, kh_read, kl_read):
        h_now = item_h[jnp.minimum(i, count - 1)]
        old = jnp.clip(i - 2, 0, count - 1)
        h_old = item_h[old]
        acc = jnp.zeros((16, leaf_size), F32)
        for c in range(0, leaf_size, rows):
            u_write[c : c + rows] = jnp.dot(a_scr[h_now, c : c + rows], b_now[...], preferred_element_type=F32)
            for r in range(c, c + rows, 16):
                high, low = halves(matern(u_read[r : r + 16]))
                kh_write[r : r + 16] = high
                kl_write[r : r + 16] = low
            acc += jnp.dot(v_scr[h_old, 0:16, c : c + rows], kh_read[c : c + rows], preferred_element_type=F32)
            acc += jnp.dot(v_scr[h_old, 16:32, c : c + rows], kl_read[c : c + rows], preferred_element_type=F32)
        target_features(i + 1, b_next)
        done = (acc[0:8] + acc[8:16]) * jnp.where((i >= 2) & (i < count + 2), GAIN, 0.0)
        at = pl.ds(pl.multiple_of((item_g[old] + (lo - base)) * leaf_size, leaf_size), leaf_size)
        out_ref[:, at] += done

    target_features(0, b0)

    def two_turns(i, _):
        turn(2 * i, b0, b1, u0, u1, kh0, kl0, kh1, kl1)
        turn(2 * i + 1, b1, b0, u1, u0, kh1, kl1, kh0, kl0)
        return 0

    lax.fori_loop(0, (count + 3) >> 1, two_turns, 0)


def near_scratch(count, slots, leaf_size):
    square = (leaf_size, leaf_size)
    leaves = count + 2 * HALO
    return [
        pltpu.VMEM((8, leaf_size), F32),
        pltpu.VMEM((leaves, 8, leaf_size), F32),
        pltpu.VMEM((leaves, leaf_size, DEPTH), BF16),
        pltpu.VMEM((leaves, 32, leaf_size), BF16),
        pltpu.VMEM((DEPTH, leaf_size), BF16),
        pltpu.VMEM((DEPTH, leaf_size), BF16),
        pltpu.VMEM(square, F32),
        pltpu.VMEM(square, F32),
        pltpu.VMEM(square, BF16),
        pltpu.VMEM(square, BF16),
        pltpu.VMEM(square, BF16),
        pltpu.VMEM(square, BF16),
        pltpu.SMEM((count * (slots + 1) + 8,), jnp.int32),
        pltpu.SMEM((count * (slots + 1) + 8,), jnp.int32),
    ]


NEAR_INPUTS = 8


def near_kernel(*refs, lo, hi, leaf_size):
    near_core(refs[:NEAR_INPUTS], refs[NEAR_INPUTS], refs[NEAR_INPUTS + 1 :], lo=lo, hi=hi, base=lo, leaf_size=leaf_size)


def near_cost(count, leaves, leaf_size):
    return pl.CostEstimate(
        flops=count * 3 * leaf_size * leaf_size * 512,
        bytes_accessed=8 * 11 * leaves * leaf_size,
        transcendentals=count * 6 * leaf_size * leaf_size,
    )


def near_specs():
    return [pl.BlockSpec(memory_space=pltpu.SMEM)] * 2 + [pl.BlockSpec(memory_space=pltpu.VMEM)] * 6


def near_field(inputs, lo, hi):
    leaves, slots = inputs[1].shape
    columns, points = inputs[3].shape
    leaf_size = points // leaves
    return pl.pallas_call(
        functools.partial(near_kernel, lo=lo, hi=hi, leaf_size=leaf_size),
        in_specs=near_specs(),
        out_specs=pl.BlockSpec(memory_space=pltpu.VMEM),
        out_shape=jax.ShapeDtypeStruct((columns, (hi - lo) * leaf_size), F32),
        scratch_shapes=near_scratch(hi - lo, slots, leaf_size),
        compiler_params=pltpu.CompilerParams(vmem_limit_bytes=NEAR_LIMIT),
        cost_estimate=near_cost(hi - lo, leaves, leaf_size),
    )(*inputs)


def last_kernel(*refs, lo, leaf_size):
    inputs = refs[:NEAR_INPUTS]
    done_ref, place_ref, target_ref, source_ref, *hbm, out_ref = refs[NEAR_INPUTS : NEAR_INPUTS + 11]
    coef, coupling, transfer, basis, down, across, local_scr, sems, *scratch = refs[NEAR_INPUTS + 11 :]
    held = (coef, coupling, transfer, basis, down, across)
    peers, slots = target_ref.shape
    leaves = basis.shape[0]
    parts = sems.shape[1]

    def copies():
        for i, (source, target) in enumerate(zip(hbm, held, strict=True)):
            number = math.gcd(parts, source.shape[0])
            size = source.shape[0] // number
            for j in range(number):
                at = pl.ds(j * size, size)
                yield pltpu.make_async_copy(source.at[at], target.at[at], sems.at[i, j])

    for copy in copies():
        copy.start()

    out_ref[:, 0 : lo * leaf_size] = done_ref[...]
    local_scr[...] = jnp.zeros_like(local_scr)
    near_core(inputs, out_ref, scratch, lo=lo, hi=leaves, base=0, leaf_size=leaf_size)

    for copy in copies():
        copy.wait()

    here = place_ref[0]
    sums = [coef[0, leaves + level] for level in range(3)]
    for p in range(1, peers):
        sums = [total + coef[p, leaves + level] for level, total in enumerate(sums)]
    region = dot_plain(sums[2], across[12 + (here >> 2)])
    region = dot_plain(sums[1], across[8 + (here >> 1)]) + dot_turned(region, down[8 + (here >> 1)])
    region = dot_plain(sums[0], across[here]) + dot_turned(region, down[here])

    def far(p, _):
        products = [dot_plain(coef[p, source_ref[p, k]], coupling[p, k]) for k in range(slots)]
        for k in range(slots):
            local_scr[target_ref[p, k]] += products[k]
        return 0

    lax.fori_loop(0, peers, far, 0)

    group = 4

    def back(i, _):
        locals_ = [local_scr[i * group + j] + dot_turned(region, transfer[i * group + j]) for j in range(group)]
        for j in range(group):
            at = pl.ds(pl.multiple_of((i * group + j) * leaf_size, leaf_size), leaf_size)
            out_ref[:, at] += dot_turned(locals_[j], basis[i * group + j])
        return 0

    lax.fori_loop(0, leaves // group, back, 0)


def last_field(inputs, done, place, targets, sources, coefs, far_coupling, leaf_transfer, leaf_basis, upper_transfer, upper_coupling):
    leaves, leaf_size, rank = leaf_basis.shape
    columns, points = inputs[3].shape
    slots = inputs[1].shape[1]
    lo = done.shape[1] // leaf_size
    smem, vmem = pl.BlockSpec(memory_space=pltpu.SMEM), pl.BlockSpec(memory_space=pltpu.VMEM)
    hbm = pl.BlockSpec(memory_space=pl.ANY)
    streamed = (coefs, far_coupling, leaf_transfer, leaf_basis, upper_transfer, upper_coupling)
    return pl.pallas_call(
        functools.partial(last_kernel, lo=lo, leaf_size=leaf_size),
        in_specs=near_specs() + [vmem, smem, smem, smem] + [hbm] * len(streamed),
        out_specs=vmem,
        out_shape=jax.ShapeDtypeStruct((columns, points), F32),
        scratch_shapes=[pltpu.VMEM(x.shape, F32) for x in streamed]
        + [pltpu.VMEM((leaves + 1, columns, rank), F32), pltpu.SemaphoreType.DMA((len(streamed), 8))]
        + near_scratch(leaves - lo, slots, leaf_size),
        compiler_params=pltpu.CompilerParams(vmem_limit_bytes=WIDE_LIMIT),
        cost_estimate=near_cost(leaves - lo, leaves, leaf_size),
    )(*inputs, done, place, targets, sources, *streamed)


def neighbours(points, vectors, width):
    axes = ("leaf", "top")
    count = lax.axis_size("leaf") * lax.axis_size("top")
    joined = [jnp.concatenate([points[:, s], vectors[:, s]], axis=0) for s in (slice(-width, None), slice(0, width))]
    before = lax.ppermute(joined[0], axes, [(i, i + 1) for i in range(count - 1)])
    after = lax.ppermute(joined[1], axes, [(i + 1, i) for i in range(count - 1)])
    return (before[:3], before[3:]), (after[:3], after[3:])


def shards(
    points,
    vectors,
    near_offset,
    leaf_basis,
    leaf_transfer,
    far_target,
    far_source,
    far_coupling,
    upper_transfer,
    upper_coupling,
):
    leaves, leaf_size, _ = leaf_basis.shape
    peers = lax.axis_size("top")
    region, peer = lax.axis_index("leaf"), lax.axis_index("top")
    place = region.astype(jnp.int32).reshape(1)
    first = ((region * peers + peer) * leaves).astype(jnp.int32).reshape(1)

    before, after = neighbours(points, vectors, HALO * leaf_size)
    coefs, parts = coefficients(place, vectors, leaf_basis, leaf_transfer, upper_transfer)
    for level, part in enumerate(siblings(parts)):
        coefs = lax.dynamic_update_slice_in_dim(coefs, part, leaves + level, 0)
    gathered = lax.all_gather(coefs, "top", axis=0)
    inputs = (first, near_offset, points, vectors, *before, *after)
    early = near_field(inputs, 0, EARLY_LEAVES)
    return last_field(
        inputs,
        early,
        place,
        far_target[0],
        far_source[0],
        gathered,
        far_coupling[0],
        leaf_transfer,
        leaf_basis,
        upper_transfer,
        upper_coupling,
    )


def solution(mesh):
    split = ("leaf", "top")
    in_specs = (
        P(None, split),
        P(None, split),
        P(split, None),
        P(split, None, None),
        P(split, None, None),
        P(split, None, None),
        P(split, None, None),
        P(split, None, None, None, None),
        P(),
        P(),
    )
    return jax.shard_map(shards, mesh=mesh, in_specs=in_specs, out_specs=P(None, split), check_vma=False)
```

time: 159 us -> 129 us (0.81)
  the two profiles are of different devices: /device:TPU:2 before, /device:TPU:56 now
where the time goes in v1:
time: 129 us
  Pallas kernels  90.9 us (70%)
  between operations  13.6 us (11%)
  starting transfers between devices  10.5 us (8%)
  waiting for transfers between devices  8.88 us (7%)
  local copies, waits for them, and re-layouts  4.02 us (3%)
    pallas_call x1, Pallas kernels, near_field(): pl.pallas_call(functools.partial(near_kernel, lo=lo, hi=hi, leaf_size=lea...  46 us
    pallas_call x1, Pallas kernels, last_field(): pl.pallas_call(functools.partial(last_kernel, lo=lo, leaf_size=leaf_size)...  37.5 us
    pallas_call x1, Pallas kernels, coefficients(): pl.pallas_call(functools.partial(coef_kernel, group=group), grid_spec=plt...  7.36 us
    ppermute x3, starting transfers between devices, from_partner(): return lax.ppermute(x, 'leaf', [(i, i ^ distance) for i in range(count)])  4.6 us
    ppermute x3, waiting for transfers between devices, from_partner(): return lax.ppermute(x, 'leaf', [(i, i ^ distance) for i in range(count)])  4.44 us
    ppermute x1, waiting for transfers between devices, neighbours(): lax.ppermute(joined[1], axes, [(i + 1, i) for i in range(count - 1)])  4.42 us
    ppermute x1, starting transfers between devices, neighbours(): lax.ppermute(joined[0], axes, [(i, i + 1) for i in range(count - 1)])  3.49 us
  transfers between devices with their start and end apart: 6, of which 4 were waited for; matrix products, arithmetic and copies ran while one was open for 2% of the time, Pallas kernels for 36%

profile of v1, /device:TPU:56, one launch (start us, length us, event | category | flops | bytes accessed | tf_op | source)
XLA Modules:
  0.0 128.6 jit_solution(11203205126140412790)
XLA Ops:
  6.5 0.0 copy-start
  6.5 0.0 copy-start.6
  6.5 0.0 copy-start.8
  6.5 0.0 copy-start.9
  6.5 0.0 copy-start.10
  6.5 0.0 all-gather.2.cloned.1.call-start
  6.6 7.4 %shard_map.101 = (f32[43,8,128]{2,1,0:T(8,128)}, f32[3,8,128]{2,1,0:T(8,128)}) custom-call(s32[1]{0:T(128)} %bitcast.1.place_ref.refs_9_, f32[8,20480]{1,0:T(8,128)} %refs_3_.3, f32[40,512,128]{2,1,0:T(8,128)} %refs_15_.1, f32[40,128,128]{2,1,0:T(8,128)} %refs_14_.1, f32[12,128,128]{2,1,0:T(8,128)} %refs_16_.1, f32[12,128,128]{2,1,0:T(8,128)} %refs_16_.1), custom_call_target="tpu_custom_call" | custom-call | flops 209715200 | bytes 13107200 | tf_op jit(solution)/shard_map/pallas_call | solution.py:100
  14.0 0.1 collective-permute-start.2
  14.1 1.4 %collective-permute-done.2 = f32[3,8,128]{2,1,0:T(8,128)S(1)} collective-permute-done((f32[3,8,128]{2,1,0:T(8,128)}, f32[3,8,128]{2,1,0:T(8,128)S(1)}, u32[]{:S(2)}, u32[]{:S(2)}) %collective-permute-start.2) | collective-permute-done | bytes 12320 | tf_op jit(solution)/shard_map/ppermute | solution.py:140
  15.4 0.7 slice_add_fusion
  16.1 1.5 %collective-permute-start.3 = (f32[2,8,128]{2,1,0:T(8,128)S(1)}, f32[2,8,128]{2,1,0:T(8,128)S(1)}, u32[]{:S(2)}, u32[]{:S(2)}) collective-permute-start(f32[2,8,128]{2,1,0:T(8,128)S(1)} %slice_add_fusion), channel_id=1, source_target_pairs={{0,32},{16,48},{32,0},{48,16},{64,96},{80,112},{96,64},{112,80},{1... | collective-permute-start | bytes 24584 | tf_op jit(solution)/shard_map/ppermute | solution.py:140
  17.6 0.6 fusion.1
  18.2 1.6 %collective-permute-done.3 = f32[2,8,128]{2,1,0:T(8,128)S(1)} collective-permute-done((f32[2,8,128]{2,1,0:T(8,128)S(1)}, f32[2,8,128]{2,1,0:T(8,128)S(1)}, u32[]{:S(2)}, u32[]{:S(2)}) %collective-permute-start.3) | collective-permute-done | bytes 8224 | tf_op jit(solution)/shard_map/ppermute | solution.py:140
  19.8 3.0 %collective-permute-start.4 = (f32[1,8,128]{2,1,0:T(8,128)S(1)}, f32[1,8,128]{2,1,0:T(8,128)S(1)}, u32[]{:S(2)}, u32[]{:S(2)}) collective-permute-start(f32[1,8,128]{2,1,0:T(8,128)S(1)} %slice_add_fusion.1), channel_id=1, source_target_pairs={{0,64},{16,80},{32,96},{48,112},{64,0},{80,16},{96,32},{112,48},{1... | collective-permute-start | bytes 12296 | tf_op jit(solution)/shard_map/ppermute | solution.py:140
  22.8 0.6 fusion
  23.4 1.5 %collective-permute-done.4 = f32[1,8,128]{2,1,0:T(8,128)S(1)} collective-permute-done((f32[1,8,128]{2,1,0:T(8,128)S(1)}, f32[1,8,128]{2,1,0:T(8,128)S(1)}, u32[]{:S(2)}, u32[]{:S(2)}) %collective-permute-start.4) | collective-permute-done | bytes 4128 | tf_op jit(solution)/shard_map/ppermute | solution.py:140
  24.9 0.6 bitcast_dynamic-update-slice_fusion
  25.5 0.0 all-gather.2.cloned.1.call-update
  25.5 0.0 copy-done.6
  25.5 0.0 copy-done
  25.6 3.5 %collective-permute-start = (f32[11,1024]{1,0:T(8,128)S(1)}, f32[11,1024]{1,0:T(8,128)S(1)}, u32[]{:S(2)}, u32[]{:S(2)}) collective-permute-start(f32[11,1024]{1,0:T(8,128)S(1)} %pad_maximum_fusion), channel_id=1, source_target_pairs={{0,1},{1,2},{2,3},{3,4},{4,5},{5,6},{6,7},{7,8},{8,9},{9,10},{10,1... | collective-permute-start | bytes 135176 | tf_op jit(solution)/shard_map/ppermute | solution.py:406
  29.1 2.4 %collective-permute-start.1 = (f32[11,1024]{1,0:T(8,128)S(1)}, f32[11,1024]{1,0:T(8,128)S(1)}, u32[]{:S(2)}, u32[]{:S(2)}) collective-permute-start(f32[11,1024]{1,0:T(8,128)S(1)} %pad_maximum_fusion.1), channel_id=1, source_target_pairs={{1,0},{2,1},{3,2},{4,3},{5,4},{6,5},{7,6},{8,7},{9,8},{10,9},{11,1... | collective-permute-start | bytes 135176 | tf_op jit(solution)/shard_map/ppermute | solution.py:407
  31.5 0.0 copy-done.8
  31.5 0.7 copy.17.refs_10_
  32.1 0.0 copy-done.9
  32.1 0.7 copy.18.refs_11_
  32.8 0.0 copy-done.10
  32.8 0.1 copy.16.refs_1_
  32.9 0.0 copy-start.3
  32.9 0.0 collective-permute-done
  32.9 0.0 copy-start.4
  32.9 0.0 copy-start.1
  33.0 4.4 %collective-permute-done.1 = f32[11,1024]{1,0:T(8,128)S(1)} collective-permute-done((f32[11,1024]{1,0:T(8,128)S(1)}, f32[11,1024]{1,0:T(8,128)S(1)}, u32[]{:S(2)}, u32[]{:S(2)}) %collective-permute-start.1) | collective-permute-done | bytes 45088 | tf_op jit(solution)/shard_map/ppermute | solution.py:407
  37.4 0.0 copy-start.5
  37.4 0.0 copy-start.2
  37.4 46.0 %shard_map.100.refs_8_ = f32[8,13312]{1,0:T(8,128)S(1)} custom-call(s32[1]{0:T(128)} %bitcast.refs_0_, s32[40,2]{1,0:T(8,128)S(1)} %copy.16.refs_1_, f32[3,20480]{1,0:T(4,128)S(1)} %copy-done.6, f32[8,20480]{1,0:T(8,128)S(1)} %copy-done, f32[3,1024]{1,0:T(4,128)S(1)} %slice.56.refs_4_, f32[8,1024]{1,0:T(8,128)S(1)} %slice.57.refs_5_, ...), custom_call_target="tpu_custom_call" | custom-call | flops 10468982784 | bytes 1802240 | tf_op jit(solution)/shard_map/pallas_call | solution.py:315
  83.4 0.0 copy-done.3
  83.4 0.0 copy-done.4
  83.4 0.0 copy-done.1
  83.4 0.0 copy-done.5
  83.5 0.0 copy-done.2
  83.5 0.0 copy-start.7
  83.5 0.8 copy-done.7
  84.2 0.0 all-gather.2.cloned.1.call-done.refs_12_
  84.2 37.5 %shard_map.102 = f32[8,20480]{1,0:T(8,128)} custom-call(s32[1]{0:T(128)} %bitcast.refs_0_, s32[40,2]{1,0:T(8,128)} %copy-done.3, f32[3,20480]{1,0:T(4,128)} %refs_2_.3, f32[8,20480]{1,0:T(8,128)} %refs_3_.3, f32[3,1024]{1,0:T(4,128)} %copy-done.4, f32[8,1024]{1,0:T(8,128)} %copy-done.1, f32[3,1024]{1,0:T(4,128)} %copy-done.5, f32[8,1024]{1,0:T(8,128)} %copy-done.2, ...), custom_call_target="tpu_custom_call" | custom-call | flops 5637144576 | bytes 1802240 | tf_op jit(solution)/shard_map/pallas_call | solution.py:389
  (9 shorter events, 0.1 us)
Async XLA Ops:
  6.5 19.0 %copy-start = (f32[8,20480]{1,0:T(8,128)S(1)}, f32[8,20480]{1,0:T(8,128)}, u32[]{:S(2)}) copy-start(f32[8,20480]{1,0:T(8,128)} %refs_3_.3) | copy-start | bytes 1966084
  6.5 19.0 %copy-start.6 = (f32[3,20480]{1,0:T(4,128)S(1)}, f32[3,20480]{1,0:T(4,128)}, u32[]{:S(2)}) copy-start(f32[3,20480]{1,0:T(4,128)} %refs_2_.3) | copy-start | bytes 737284
  6.5 24.9 %copy-start.8 = (s32[1,16,8]{1,2,0:T(8,128)S(1)}, s32[1,16,8]{1,2,0:T(8,128)}, u32[]{:S(2)}) copy-start(s32[1,16,8]{1,2,0:T(8,128)} %param.15) | copy-start | bytes 1540
  6.5 25.6 %copy-start.9 = (s32[1,16,8]{1,2,0:T(8,128)S(1)}, s32[1,16,8]{1,2,0:T(8,128)}, u32[]{:S(2)}) copy-start(s32[1,16,8]{1,2,0:T(8,128)} %param.16) | copy-start | bytes 1540
  6.5 26.3 %copy-start.10 = (s32[40,2]{0,1:T(2,128)S(1)}, s32[40,2]{0,1:T(2,128)}, u32[]{:S(2)}) copy-start(s32[40,2]{0,1:T(2,128)} %param.12) | copy-start | bytes 964
  6.5 77.7 %all-gather.2.cloned.1.call-start = ((), (), s32[]{:S(2)}) async-start(), calls=%async_computation | async-start | bytes 2994176 | tf_op jit(solution)/shard_map/all_gather | solution.py:433
  14.0 1.5 %collective-permute-start.2 = (f32[3,8,128]{2,1,0:T(8,128)}, f32[3,8,128]{2,1,0:T(8,128)S(1)}, u32[]{:S(2)}, u32[]{:S(2)}) collective-permute-start(f32[3,8,128]{2,1,0:T(8,128)} %get-tuple-element.8), channel_id=1, source_target_pairs={{0,16},{16,0},{32,48},{48,32},{64,80},{80,64},{96,112},{112,96},{1... | collective-permute-start | bytes 36872 | tf_op jit(solution)/shard_map/ppermute | solution.py:140
  16.1 3.7 %collective-permute-start.3 = (f32[2,8,128]{2,1,0:T(8,128)S(1)}, f32[2,8,128]{2,1,0:T(8,128)S(1)}, u32[]{:S(2)}, u32[]{:S(2)}) collective-permute-start(f32[2,8,128]{2,1,0:T(8,128)S(1)} %slice_add_fusion), channel_id=1, source_target_pairs={{0,32},{16,48},{32,0},{48,16},{64,96},{80,112},{96,64},{112,80},{1... | collective-permute-start | bytes 24584 | tf_op jit(solution)/shard_map/ppermute | solution.py:140
  19.8 5.1 %collective-permute-start.4 = (f32[1,8,128]{2,1,0:T(8,128)S(1)}, f32[1,8,128]{2,1,0:T(8,128)S(1)}, u32[]{:S(2)}, u32[]{:S(2)}) collective-permute-start(f32[1,8,128]{2,1,0:T(8,128)S(1)} %slice_add_fusion.1), channel_id=1, source_target_pairs={{0,64},{16,80},{32,96},{48,112},{64,0},{80,16},{96,32},{112,48},{1... | collective-permute-start | bytes 12296 | tf_op jit(solution)/shard_map/ppermute | solution.py:140
  25.6 7.3 %collective-permute-start = (f32[11,1024]{1,0:T(8,128)S(1)}, f32[11,1024]{1,0:T(8,128)S(1)}, u32[]{:S(2)}, u32[]{:S(2)}) collective-permute-start(f32[11,1024]{1,0:T(8,128)S(1)} %pad_maximum_fusion), channel_id=1, source_target_pairs={{0,1},{1,2},{2,3},{3,4},{4,5},{5,6},{6,7},{7,8},{8,9},{9,10},{10,1... | collective-permute-start | bytes 135176 | tf_op jit(solution)/shard_map/ppermute | solution.py:406
  29.1 8.3 %collective-permute-start.1 = (f32[11,1024]{1,0:T(8,128)S(1)}, f32[11,1024]{1,0:T(8,128)S(1)}, u32[]{:S(2)}, u32[]{:S(2)}) collective-permute-start(f32[11,1024]{1,0:T(8,128)S(1)} %pad_maximum_fusion.1), channel_id=1, source_target_pairs={{1,0},{2,1},{3,2},{4,3},{5,4},{6,5},{7,6},{8,7},{9,8},{10,9},{11,1... | collective-permute-start | bytes 135176 | tf_op jit(solution)/shard_map/ppermute | solution.py:407
  32.9 50.5 %copy-start.3 = (s32[40,2]{1,0:T(8,128)}, s32[40,2]{1,0:T(8,128)S(1)}, u32[]{:S(2)}) copy-start(s32[40,2]{1,0:T(8,128)S(1)} %copy.16.refs_1_) | copy-start | bytes 964
  32.9 50.5 %copy-start.4 = (f32[3,1024]{1,0:T(4,128)}, f32[3,1024]{1,0:T(4,128)S(1)}, u32[]{:S(2)}) copy-start(f32[3,1024]{1,0:T(4,128)S(1)} %slice.56.refs_4_) | copy-start | bytes 36868
  32.9 50.5 %copy-start.1 = (f32[8,1024]{1,0:T(8,128)}, f32[8,1024]{1,0:T(8,128)S(1)}, u32[]{:S(2)}) copy-start(f32[8,1024]{1,0:T(8,128)S(1)} %slice.57.refs_5_) | copy-start | bytes 98308
  37.4 46.1 %copy-start.5 = (f32[3,1024]{1,0:T(4,128)}, f32[3,1024]{1,0:T(4,128)S(1)}, u32[]{:S(2)}) copy-start(f32[3,1024]{1,0:T(4,128)S(1)} %slice.58.refs_6_) | copy-start | bytes 36868
  37.4 46.1 %copy-start.2 = (f32[8,1024]{1,0:T(8,128)}, f32[8,1024]{1,0:T(8,128)S(1)}, u32[]{:S(2)}) copy-start(f32[8,1024]{1,0:T(8,128)S(1)} %slice.59.refs_7_) | copy-start | bytes 98308
  83.5 0.8 copy-start.7
Sparse Core Ops, SparseCore 0:
  25.6 47.0 all-gather.1

commit v2 on v1

--- a/solution.py
+++ b/solution.py
@@ -17,9 +17,11 @@
 TINY = 1e-20
 DEPTH = 64
 HALO = 2
+CHUNK = 64
+UNROLL = 4
 NEAR_LIMIT = 20 << 20
 WIDE_LIMIT = 56 << 20
-EARLY_LEAVES = 26
+EARLY_LEAVES = 30
 
 
 def halves(x):
@@ -133,19 +135,6 @@
     )(place, vectors, leaf_basis, leaf_transfer, upper_transfer, upper_transfer)
 
 
-def siblings(parts):
-    count = lax.axis_size("leaf")
-
-    def from_partner(x, distance):
-        return lax.ppermute(x, "leaf", [(i, i ^ distance) for i in range(count)])
-
-    other = from_partner(parts, 1)
-    level0, parts = other[0:1], parts[1:] + other[1:]
-    other = from_partner(parts, 2)
-    level1, parts = other[0:1], parts[1:] + other[1:]
-    return level0, level1, from_partner(parts, 4)
-
-
 def features(x, target):
     row = lax.broadcasted_iota(jnp.int32, x.shape, 0)
     norm = jnp.sum(x * x, axis=0, keepdims=True)
@@ -169,28 +158,17 @@
 
 
 def matern(dist_sq):
-    dist_sq = jnp.maximum(dist_sq, TINY)
     nt = -LOG2E - dist_sq * lax.rsqrt(dist_sq)
     return nt * jnp.exp2(nt)
 
 
 def near_core(inputs, out_ref, scratch, *, lo, hi, base, leaf_size):
     first_ref, offset_ref, points_ref, vectors_ref, before_p, before_v, after_p, after_v = inputs
-    wide_scr, x_scr, a_scr, v_scr, b0, b1, u0, u1, kh0, kh1, kl0, kl1, item_g, item_h = scratch
-    rows = leaf_size // 2
+    wide_scr, x_scr, a_scr, v_scr, b0, b1, u_scr, kh_scr, kl_scr, item_g, item_h = scratch
     leaves = offset_ref.shape[0]
     first = first_ref[0]
     row8 = lax.broadcasted_iota(jnp.int32, (8, leaf_size), 0)
 
-    def clear(ref):
-        def turn(i, _):
-            ref[pl.ds(pl.multiple_of(i * 16, 16), 16)] = jnp.zeros((16, leaf_size), ref.dtype)
-            return 0
-
-        lax.fori_loop(0, leaf_size // 16, turn, 0)
-
-    for ref in (u0, u1, kh0, kh1, kl0, kl1):
-        clear(ref)
     wide_scr[...] = jnp.zeros_like(wide_scr)
 
     def prepare(p_ref, v_ref, start, stop, origin):
@@ -240,32 +218,40 @@
         x = x_scr[g + HALO]
         b_scr[...] = features(jnp.where(row8 == 0, x + apart, x), True).astype(BF16)
 
-    def turn(i, b_now, b_next, u_write, u_read, kh_write, kl_write, kh_read, kl_read):
-        h_now = item_h[jnp.minimum(i, count - 1)]
-        old = jnp.clip(i - 2, 0, count - 1)
-        h_old = item_h[old]
+    def distances(i, b_scr, c, size):
+        h = item_h[jnp.minimum(i, count - 1)]
+        dist_sq = jnp.dot(a_scr[h, c : c + size], b_scr[...], preferred_element_type=F32)
+        u_scr[c : c + size] = jnp.maximum(dist_sq, TINY)
+
+    def turn(i, b_next, b_later):
+        now = jnp.minimum(i, count - 1)
+        h = item_h[now]
         acc = jnp.zeros((16, leaf_size), F32)
-        for c in range(0, leaf_size, rows):
-            u_write[c : c + rows] = jnp.dot(a_scr[h_now, c : c + rows], b_now[...], preferred_element_type=F32)
-            for r in range(c, c + rows, 16):
-                high, low = halves(matern(u_read[r : r + 16]))
-                kh_write[r : r + 16] = high
-                kl_write[r : r + 16] = low
-            acc += jnp.dot(v_scr[h_old, 0:16, c : c + rows], kh_read[c : c + rows], preferred_element_type=F32)
-            acc += jnp.dot(v_scr[h_old, 16:32, c : c + rows], kl_read[c : c + rows], preferred_element_type=F32)
-        target_features(i + 1, b_next)
-        done = (acc[0:8] + acc[8:16]) * jnp.where((i >= 2) & (i < count + 2), GAIN, 0.0)
-        at = pl.ds(pl.multiple_of((item_g[old] + (lo - base)) * leaf_size, leaf_size), leaf_size)
+        size = CHUNK
+        for c in range(0, leaf_size, size):
+            for r in range(c, c + size, 32):
+                high, low = halves(matern(u_scr[r : r + 32]))
+                kh_scr[r : r + 32] = high
+                kl_scr[r : r + 32] = low
+            distances(i + 1, b_next, c, size)
+            acc += jnp.dot(v_scr[h, 0:16, c : c + size], kh_scr[c : c + size], preferred_element_type=F32)
+            acc += jnp.dot(v_scr[h, 16:32, c : c + size], kl_scr[c : c + size], preferred_element_type=F32)
+        target_features(i + 2, b_later)
+        done = jnp.where(i < count, (acc[0:8] + acc[8:16]) * GAIN, 0.0)
+        at = pl.ds(pl.multiple_of((item_g[now] + (lo - base)) * leaf_size, leaf_size), leaf_size)
         out_ref[:, at] += done
 
     target_features(0, b0)
-
-    def two_turns(i, _):
-        turn(2 * i, b0, b1, u0, u1, kh0, kl0, kh1, kl1)
-        turn(2 * i + 1, b1, b0, u1, u0, kh1, kl1, kh0, kl0)
+    target_features(1, b1)
+    distances(0, b0, 0, leaf_size)
+
+    def turns(i, _):
+        for j in range(0, UNROLL, 2):
+            turn(UNROLL * i + j, b1, b0)
+            turn(UNROLL * i + j + 1, b0, b1)
         return 0
 
-    lax.fori_loop(0, (count + 3) >> 1, two_turns, 0)
+    lax.fori_loop(0, (count + (UNROLL - 1)) >> UNROLL.bit_length() - 1, turns, 0)
 
 
 def near_scratch(count, slots, leaf_size):
@@ -279,9 +265,6 @@
         pltpu.VMEM((DEPTH, leaf_size), BF16),
         pltpu.VMEM((DEPTH, leaf_size), BF16),
         pltpu.VMEM(square, F32),
-        pltpu.VMEM(square, F32),
-        pltpu.VMEM(square, BF16),
-        pltpu.VMEM(square, BF16),
         pltpu.VMEM(square, BF16),
         pltpu.VMEM(square, BF16),
         pltpu.SMEM((count * (slots + 1) + 8,), jnp.int32),
@@ -399,13 +382,26 @@
     )(*inputs, done, place, targets, sources, *streamed)
 
 
-def neighbours(points, vectors, width):
+def exchange(points, vectors, parts, width):
     axes = ("leaf", "top")
-    count = lax.axis_size("leaf") * lax.axis_size("top")
-    joined = [jnp.concatenate([points[:, s], vectors[:, s]], axis=0) for s in (slice(-width, None), slice(0, width))]
-    before = lax.ppermute(joined[0], axes, [(i, i + 1) for i in range(count - 1)])
-    after = lax.ppermute(joined[1], axes, [(i + 1, i) for i in range(count - 1)])
-    return (before[:3], before[3:]), (after[:3], after[3:])
+    regions = lax.axis_size("leaf")
+    count = regions * lax.axis_size("top")
+    head, tail = (jnp.concatenate([points[:, s], vectors[:, s]], axis=0) for s in (slice(0, width), slice(-width, None)))
+
+    def from_partner(x, distance):
+        return lax.ppermute(x, "leaf", [(i, i ^ distance) for i in range(regions)])
+
+    parts, head, tail = lax.optimization_barrier((parts, head, tail))
+    before = lax.ppermute(tail, axes, [(i, i + 1) for i in range(count - 1)])
+    other = from_partner(parts, 1)
+    before, other, head = lax.optimization_barrier((before, other, head))
+    level0, parts = other[0:1], parts[1:] + other[1:]
+    after = lax.ppermute(head, axes, [(i + 1, i) for i in range(count - 1)])
+    other = from_partner(parts, 2)
+    after, other = lax.optimization_barrier((after, other))
+    level1, parts = other[0:1], parts[1:] + other[1:]
+    level2 = from_partner(parts, 4)
+    return (before[:3], before[3:]), (after[:3], after[3:]), (level0, level1, level2)
 
 
 def shards(
@@ -426,10 +422,9 @@
     place = region.astype(jnp.int32).reshape(1)
     first = ((region * peers + peer) * leaves).astype(jnp.int32).reshape(1)
 
-    before, after = neighbours(points, vectors, HALO * leaf_size)
     coefs, parts = coefficients(place, vectors, leaf_basis, leaf_transfer, upper_transfer)
-    for level, part in enumerate(siblings(parts)):
-        coefs = lax.dynamic_update_slice_in_dim(coefs, part, leaves + level, 0)
+    before, after, levels = exchange(points, vectors, parts, HALO * leaf_size)
+    coefs = lax.dynamic_update_slice_in_dim(coefs, jnp.concatenate(levels), leaves, 0)
     gathered = lax.all_gather(coefs, "top", axis=0)
     inputs = (first, near_offset, points, vectors, *before, *after)
     early = near_field(inputs, 0, EARLY_LEAVES)

time: 129 us -> 119 us (0.922)
  the two profiles are of different devices: /device:TPU:56 before, /device:TPU:4 now
where the time goes in v2:
time: 119 us
  Pallas kernels  73.8 us (62%)
  waiting for transfers between devices  18 us (15%)
  between operations  13.6 us (11%)
  starting transfers between devices  8.1 us (7%)
  local copies, waits for them, and re-layouts  3.84 us (3%)
  other arithmetic  1.32 us (1%)
    pallas_call x1, Pallas kernels, near_field(): pl.pallas_call(functools.partial(near_kernel, lo=lo, hi=hi, leaf_size=lea...  40.8 us
    pallas_call x1, Pallas kernels, last_field(): pl.pallas_call(functools.partial(last_kernel, lo=lo, leaf_size=leaf_size)...  25.7 us
    ppermute x3, waiting for transfers between devices, from_partner(): return lax.ppermute(x, 'leaf', [(i, i ^ distance) for i in range(regions)])  8.63 us
    pallas_call x1, Pallas kernels, coefficients(): pl.pallas_call(functools.partial(coef_kernel, group=group), grid_spec=plt...  7.27 us
    ppermute x1, waiting for transfers between devices, exchange(): before = lax.ppermute(tail, axes, [(i, i + 1) for i in range(count - 1)])  4.84 us
    all_gather x1, waiting for transfers between devices, shards(): gathered = lax.all_gather(coefs, 'top', axis=0)  4.53 us
    ppermute x1, starting transfers between devices, exchange(): before = lax.ppermute(tail, axes, [(i, i + 1) for i in range(count - 1)])  3.48 us
    ppermute x1, starting transfers between devices, exchange(): after = lax.ppermute(head, axes, [(i + 1, i) for i in range(count - 1)])  3 us
  transfers between devices with their start and end apart: 6, of which 5 were waited for; matrix products, arithmetic and copies ran while one was open for 2% of the time, Pallas kernels for 34%

profile of v2, /device:TPU:4, one launch (start us, length us, event | category | flops | bytes accessed | tf_op | source)
XLA Modules:
  0.0 118.7 jit_solution(13127333969733395602)
XLA Ops:
  6.5 0.0 copy-start.6
  6.5 0.0 copy-start
  6.5 0.0 copy-start.8
  6.5 0.0 copy-start.9
  6.5 0.0 copy-start.10
  6.5 0.0 all-gather.2.cloned.1.call-start
  6.6 0.8 fusion.2
  7.4 0.8 fusion.1
  8.2 7.3 %shard_map.100 = (f32[43,8,128]{2,1,0:T(8,128)}, f32[3,8,128]{2,1,0:T(8,128)}) custom-call(s32[1]{0:T(128)} %bitcast.1.place_ref.refs_9_, f32[8,20480]{1,0:T(8,128)} %refs_3_.3, f32[40,512,128]{2,1,0:T(8,128)} %refs_15_.1, f32[40,128,128]{2,1,0:T(8,128)} %refs_14_.1, f32[12,128,128]{2,1,0:T(8,128)} %refs_16_.1, f32[12,128,128]{2,1,0:T(8,128)} %refs_16_.1), custom_call_target="tpu_custom_call" | custom-call | flops 209715200 | bytes 13107200 | tf_op jit(solution)/shard_map/pallas_call | solution.py:102
  15.5 3.5 %collective-permute-start = (f32[11,1024]{1,0:T(8,128)S(1)}, f32[11,1024]{1,0:T(8,128)S(1)}, u32[]{:S(2)}, u32[]{:S(2)}) collective-permute-start(f32[11,1024]{1,0:T(8,128)S(1)} %get-tuple-element.16), channel_id=1, source_target_pairs={{0,1},{1,2},{2,3},{3,4},{4,5},{5,6},{6,7},{7,8},{8,9},{9,10},{10,1... | collective-permute-start | bytes 135176 | tf_op jit(solution)/shard_map/ppermute | solution.py:395
  19.0 0.1 collective-permute-start.1
  19.1 1.4 %collective-permute-done.1 = f32[3,8,128]{2,1,0:T(8,128)S(1)} collective-permute-done((f32[3,8,128]{2,1,0:T(8,128)}, f32[3,8,128]{2,1,0:T(8,128)S(1)}, u32[]{:S(2)}, u32[]{:S(2)}) %collective-permute-start.1) | collective-permute-done | bytes 12320 | tf_op jit(solution)/shard_map/ppermute | solution.py:392
  20.5 4.8 %collective-permute-done = f32[11,1024]{1,0:T(8,128)S(1)} collective-permute-done((f32[11,1024]{1,0:T(8,128)S(1)}, f32[11,1024]{1,0:T(8,128)S(1)}, u32[]{:S(2)}, u32[]{:S(2)}) %collective-permute-start) | collective-permute-done | bytes 45088 | tf_op jit(solution)/shard_map/ppermute | solution.py:395
  25.3 3.0 %collective-permute-start.2 = (f32[11,1024]{1,0:T(8,128)S(1)}, f32[11,1024]{1,0:T(8,128)S(1)}, u32[]{:S(2)}, u32[]{:S(2)}) collective-permute-start(f32[11,1024]{1,0:T(8,128)S(1)} %get-tuple-element.20), channel_id=1, source_target_pairs={{1,0},{2,1},{3,2},{4,3},{5,4},{6,5},{7,6},{8,7},{9,8},{10,9},{11,1... | collective-permute-start | bytes 135176 | tf_op jit(solution)/shard_map/ppermute | solution.py:399
  28.3 0.7 slice_add_fusion
  29.0 1.5 %collective-permute-start.3 = (f32[2,8,128]{2,1,0:T(8,128)S(1)}, f32[2,8,128]{2,1,0:T(8,128)S(1)}, u32[]{:S(2)}, u32[]{:S(2)}) collective-permute-start(f32[2,8,128]{2,1,0:T(8,128)S(1)} %slice_add_fusion), channel_id=1, source_target_pairs={{0,32},{16,48},{32,0},{48,16},{64,96},{80,112},{96,64},{112,80},{1... | collective-permute-start | bytes 24584 | tf_op jit(solution)/shard_map/ppermute | solution.py:392
  30.5 2.2 %collective-permute-done.3 = f32[2,8,128]{2,1,0:T(8,128)S(1)} collective-permute-done((f32[2,8,128]{2,1,0:T(8,128)S(1)}, f32[2,8,128]{2,1,0:T(8,128)S(1)}, u32[]{:S(2)}, u32[]{:S(2)}) %collective-permute-start.3) | collective-permute-done | bytes 8224 | tf_op jit(solution)/shard_map/ppermute | solution.py:392
  32.7 0.0 collective-permute-done.2
  32.7 0.0 collective-permute-start.4
  32.7 5.1 %collective-permute-done.4 = f32[1,8,128]{2,1,0:T(8,128)S(1)} collective-permute-done((f32[1,8,128]{2,1,0:T(8,128)S(1)}, f32[1,8,128]{2,1,0:T(8,128)S(1)}, u32[]{:S(2)}, u32[]{:S(2)}) %collective-permute-start.4) | collective-permute-done | bytes 4128 | tf_op jit(solution)/shard_map/ppermute | solution.py:392
  37.8 0.6 fusion
  38.4 0.0 all-gather.2.cloned.1.call-update
  38.4 0.0 copy-done.8
  38.4 0.7 copy.17.refs_10_
  39.1 0.0 copy-done.9
  39.1 0.7 copy.18.refs_11_
  39.8 0.0 copy-done.10
  39.8 0.1 copy.16.refs_1_
  39.8 0.0 copy-start.3
  39.9 0.0 copy-start.4
  39.9 0.0 copy-start.1
  39.9 0.0 copy-start.5
  39.9 0.0 copy-start.2
  39.9 0.0 copy-done.6
  39.9 0.0 copy-done
  40.0 40.8 %shard_map.101.refs_8_ = f32[8,15360]{1,0:T(8,128)S(1)} custom-call(s32[1]{0:T(128)} %bitcast.refs_0_, s32[40,2]{1,0:T(8,128)S(1)} %copy.16.refs_1_, f32[3,20480]{1,0:T(4,128)S(1)} %copy-done.6, f32[8,20480]{1,0:T(8,128)S(1)} %copy-done, f32[3,1024]{1,0:T(4,128)S(1)} %slice.46.refs_4_, f32[8,1024]{1,0:T(8,128)S(1)} %slice.47.refs_5_, ...), custom_call_target="tpu_custom_call" | custom-call | flops 12079595520 | bytes 1802240 | tf_op jit(solution)/shard_map/pallas_call | solution.py:298
  80.8 0.0 copy-done.3
  80.8 0.0 copy-done.4
  80.8 0.0 copy-done.1
  80.8 0.0 copy-done.5
  80.8 0.0 copy-done.2
  80.8 0.0 copy-start.7
  80.9 0.8 copy-done.7
  81.6 4.5 %all-gather.2.cloned.1.call-done.refs_12_ = f32[16,43,8,128]{3,2,1,0:T(8,128)} async-done(((f32[1,43,8,128]{3,2,1,0:T(8,128)}), f32[16,43,8,128]{3,2,1,0:T(8,128)}) %all-gather.2.cloned.1.call-update) | async-done | bytes 2818064 | tf_op jit(solution)/shard_map/all_gather | solution.py:428
  86.1 25.7 %shard_map.102 = f32[8,20480]{1,0:T(8,128)} custom-call(s32[1]{0:T(128)} %bitcast.refs_0_, s32[40,2]{1,0:T(8,128)} %copy-done.3, f32[3,20480]{1,0:T(4,128)} %refs_2_.3, f32[8,20480]{1,0:T(8,128)} %refs_3_.3, f32[3,1024]{1,0:T(4,128)} %copy-done.4, f32[8,1024]{1,0:T(8,128)} %copy-done.1, f32[3,1024]{1,0:T(4,128)} %copy-done.5, f32[8,1024]{1,0:T(8,128)} %copy-done.2, ...), custom_call_target="tpu_custom_call" | custom-call | flops 4026531840 | bytes 1802240 | tf_op jit(solution)/shard_map/pallas_call | solution.py:372
  (7 shorter events, 0.0 us)
Async XLA Ops:
  6.5 33.4 %copy-start.6 = (f32[3,20480]{1,0:T(4,128)S(1)}, f32[3,20480]{1,0:T(4,128)}, u32[]{:S(2)}) copy-start(f32[3,20480]{1,0:T(4,128)} %refs_2_.3) | copy-start | bytes 737284
  6.5 33.4 %copy-start = (f32[8,20480]{1,0:T(8,128)S(1)}, f32[8,20480]{1,0:T(8,128)}, u32[]{:S(2)}) copy-start(f32[8,20480]{1,0:T(8,128)} %refs_3_.3) | copy-start | bytes 1966084
  6.5 31.9 %copy-start.8 = (s32[1,16,8]{1,2,0:T(8,128)S(1)}, s32[1,16,8]{1,2,0:T(8,128)}, u32[]{:S(2)}) copy-start(s32[1,16,8]{1,2,0:T(8,128)} %param.15) | copy-start | bytes 1540
  6.5 32.6 %copy-start.9 = (s32[1,16,8]{1,2,0:T(8,128)S(1)}, s32[1,16,8]{1,2,0:T(8,128)}, u32[]{:S(2)}) copy-start(s32[1,16,8]{1,2,0:T(8,128)} %param.16) | copy-start | bytes 1540
  6.5 33.2 %copy-start.10 = (s32[40,2]{0,1:T(2,128)S(1)}, s32[40,2]{0,1:T(2,128)}, u32[]{:S(2)}) copy-start(s32[40,2]{0,1:T(2,128)} %param.12) | copy-start | bytes 964
  6.5 79.6 %all-gather.2.cloned.1.call-start = ((), (), s32[]{:S(2)}) async-start(), calls=%async_computation | async-start | bytes 2994176 | tf_op jit(solution)/shard_map/all_gather | solution.py:428
  15.5 9.8 %collective-permute-start = (f32[11,1024]{1,0:T(8,128)S(1)}, f32[11,1024]{1,0:T(8,128)S(1)}, u32[]{:S(2)}, u32[]{:S(2)}) collective-permute-start(f32[11,1024]{1,0:T(8,128)S(1)} %get-tuple-element.16), channel_id=1, source_target_pairs={{0,1},{1,2},{2,3},{3,4},{4,5},{5,6},{6,7},{7,8},{8,9},{9,10},{10,1... | collective-permute-start | bytes 135176 | tf_op jit(solution)/shard_map/ppermute | solution.py:395
  19.0 1.5 %collective-permute-start.1 = (f32[3,8,128]{2,1,0:T(8,128)}, f32[3,8,128]{2,1,0:T(8,128)S(1)}, u32[]{:S(2)}, u32[]{:S(2)}) collective-permute-start(f32[3,8,128]{2,1,0:T(8,128)} %get-tuple-element.17), channel_id=1, source_target_pairs={{0,16},{16,0},{32,48},{48,32},{64,80},{80,64},{96,112},{112,96},{1... | collective-permute-start | bytes 36872 | tf_op jit(solution)/shard_map/ppermute | solution.py:392
  25.3 7.4 %collective-permute-start.2 = (f32[11,1024]{1,0:T(8,128)S(1)}, f32[11,1024]{1,0:T(8,128)S(1)}, u32[]{:S(2)}, u32[]{:S(2)}) collective-permute-start(f32[11,1024]{1,0:T(8,128)S(1)} %get-tuple-element.20), channel_id=1, source_target_pairs={{1,0},{2,1},{3,2},{4,3},{5,4},{6,5},{7,6},{8,7},{9,8},{10,9},{11,1... | collective-permute-start | bytes 135176 | tf_op jit(solution)/shard_map/ppermute | solution.py:399
  29.0 3.7 %collective-permute-start.3 = (f32[2,8,128]{2,1,0:T(8,128)S(1)}, f32[2,8,128]{2,1,0:T(8,128)S(1)}, u32[]{:S(2)}, u32[]{:S(2)}) collective-permute-start(f32[2,8,128]{2,1,0:T(8,128)S(1)} %slice_add_fusion), channel_id=1, source_target_pairs={{0,32},{16,48},{32,0},{48,16},{64,96},{80,112},{96,64},{112,80},{1... | collective-permute-start | bytes 24584 | tf_op jit(solution)/shard_map/ppermute | solution.py:392
  32.7 5.1 %collective-permute-start.4 = (f32[1,8,128]{2,1,0:T(8,128)S(1)}, f32[1,8,128]{2,1,0:T(8,128)S(1)}, u32[]{:S(2)}, u32[]{:S(2)}) collective-permute-start(f32[1,8,128]{2,1,0:T(8,128)S(1)} %get-tuple-element.30), channel_id=1, source_target_pairs={{0,64},{16,80},{32,96},{48,112},{64,0},{80,16},{96,32},{112,48},{1... | collective-permute-start | bytes 12296 | tf_op jit(solution)/shard_map/ppermute | solution.py:392
  39.8 41.0 %copy-start.3 = (s32[40,2]{1,0:T(8,128)}, s32[40,2]{1,0:T(8,128)S(1)}, u32[]{:S(2)}) copy-start(s32[40,2]{1,0:T(8,128)S(1)} %copy.16.refs_1_) | copy-start | bytes 964
  39.9 41.0 %copy-start.4 = (f32[3,1024]{1,0:T(4,128)}, f32[3,1024]{1,0:T(4,128)S(1)}, u32[]{:S(2)}) copy-start(f32[3,1024]{1,0:T(4,128)S(1)} %slice.46.refs_4_) | copy-start | bytes 36868
  39.9 40.9 %copy-start.1 = (f32[8,1024]{1,0:T(8,128)}, f32[8,1024]{1,0:T(8,128)S(1)}, u32[]{:S(2)}) copy-start(f32[8,1024]{1,0:T(8,128)S(1)} %slice.47.refs_5_) | copy-start | bytes 98308
  39.9 40.9 %copy-start.5 = (f32[3,1024]{1,0:T(4,128)}, f32[3,1024]{1,0:T(4,128)S(1)}, u32[]{:S(2)}) copy-start(f32[3,1024]{1,0:T(4,128)S(1)} %slice.50.refs_6_) | copy-start | bytes 36868
  39.9 40.9 %copy-start.2 = (f32[8,1024]{1,0:T(8,128)}, f32[8,1024]{1,0:T(8,128)S(1)}, u32[]{:S(2)}) copy-start(f32[8,1024]{1,0:T(8,128)S(1)} %slice.51.refs_7_) | copy-start | bytes 98308
  80.8 0.8 copy-start.7
Sparse Core Ops, SparseCore 0:
  38.5 47.5 all-gather.1

commit v3 on v2

--- a/solution.py
+++ b/solution.py
@@ -21,7 +21,8 @@
 UNROLL = 4
 NEAR_LIMIT = 20 << 20
 WIDE_LIMIT = 56 << 20
-EARLY_LEAVES = 30
+LAST_LIMIT = 56 << 20
+EARLY_LEAVES = 32
 
 
 def halves(x):
@@ -56,7 +57,7 @@
     return out[0:8] + out[8:16]
 
 
-def coef_kernel(place_ref, vec_hbm, basis_hbm, transfer_hbm, up0_ref, up1_ref, coef_ref, part_ref, vec, basis, transfer, sems, *, group):
+def coef_kernel(place_ref, vec_hbm, basis_hbm, transfer_hbm, up0_ref, up1_ref, coef_ref, vec, basis, transfer, sems, *, group):
     del place_ref
     leaves, leaf_size, _ = basis.shape
     groups = leaves // group
@@ -86,11 +87,11 @@
             total += dot_plain(coefs[j], transfer[i * group + j])
         return total
 
-    part = lax.fori_loop(0, groups, turn, jnp.zeros(part_ref.shape[1:], F32))
-    part_ref[0] = part
+    part = lax.fori_loop(0, groups, turn, jnp.zeros(coef_ref.shape[1:], F32))
+    coef_ref[leaves] = part
     part = dot_plain(part, up0_ref[0])
-    part_ref[1] = part
-    part_ref[2] = dot_plain(part, up1_ref[0])
+    coef_ref[leaves + 1] = part
+    coef_ref[leaves + 2] = dot_plain(part, up1_ref[0])
 
 
 def coefficients(place, vectors, leaf_basis, leaf_transfer, upper_transfer):
@@ -111,10 +112,7 @@
                 pl.BlockSpec(node, lambda i, p: (p[0], 0, 0)),
                 pl.BlockSpec(node, lambda i, p: (8 + (p[0] >> 1), 0, 0)),
             ],
-            out_specs=[
-                pl.BlockSpec((leaves + 3, columns, rank), lambda i, p: (0, 0, 0)),
-                pl.BlockSpec((3, columns, rank), lambda i, p: (0, 0, 0)),
-            ],
+            out_specs=pl.BlockSpec((leaves + 3, columns, rank), lambda i, p: (0, 0, 0)),
             scratch_shapes=[
                 pltpu.VMEM(vectors.shape, F32),
                 pltpu.VMEM(leaf_basis.shape, F32),
@@ -122,10 +120,7 @@
                 pltpu.SemaphoreType.DMA((3, leaves // group)),
             ],
         ),
-        out_shape=[
-            jax.ShapeDtypeStruct((leaves + 3, columns, rank), F32),
-            jax.ShapeDtypeStruct((3, columns, rank), F32),
-        ],
+        out_shape=jax.ShapeDtypeStruct((leaves + 3, columns, rank), F32),
         compiler_params=pltpu.CompilerParams(vmem_limit_bytes=WIDE_LIMIT),
         cost_estimate=pl.CostEstimate(
             flops=leaves * 16 * rank * (leaf_size + rank) * 4,
@@ -308,10 +303,10 @@
 
 def last_kernel(*refs, lo, leaf_size):
     inputs = refs[:NEAR_INPUTS]
-    done_ref, place_ref, target_ref, source_ref, *hbm, out_ref = refs[NEAR_INPUTS : NEAR_INPUTS + 11]
-    coef, coupling, transfer, basis, down, across, local_scr, sems, *scratch = refs[NEAR_INPUTS + 11 :]
+    done_ref, place_ref, slot_ref, level0, level1, level2, *hbm, out_ref = refs[NEAR_INPUTS : NEAR_INPUTS + 13]
+    coef, coupling, transfer, basis, down, across, local_scr, sems, *scratch = refs[NEAR_INPUTS + 13 :]
     held = (coef, coupling, transfer, basis, down, across)
-    peers, slots = target_ref.shape
+    peers, slots, _, _ = coupling.shape
     leaves = basis.shape[0]
     parts = sems.shape[1]
 
@@ -334,17 +329,14 @@
         copy.wait()
 
     here = place_ref[0]
-    sums = [coef[0, leaves + level] for level in range(3)]
-    for p in range(1, peers):
-        sums = [total + coef[p, leaves + level] for level, total in enumerate(sums)]
-    region = dot_plain(sums[2], across[12 + (here >> 2)])
-    region = dot_plain(sums[1], across[8 + (here >> 1)]) + dot_turned(region, down[8 + (here >> 1)])
-    region = dot_plain(sums[0], across[here]) + dot_turned(region, down[here])
+    region = dot_plain(level2[0], across[12 + (here >> 2)])
+    region = dot_plain(level1[0], across[8 + (here >> 1)]) + dot_turned(region, down[8 + (here >> 1)])
+    region = dot_plain(level0[0], across[here]) + dot_turned(region, down[here])
 
     def far(p, _):
-        products = [dot_plain(coef[p, source_ref[p, k]], coupling[p, k]) for k in range(slots)]
+        products = [dot_plain(coef[p, slot_ref[peers + p, k]], coupling[p, k]) for k in range(slots)]
         for k in range(slots):
-            local_scr[target_ref[p, k]] += products[k]
+            local_scr[slot_ref[p, k]] += products[k]
         return 0
 
     lax.fori_loop(0, peers, far, 0)
@@ -361,7 +353,7 @@
     lax.fori_loop(0, leaves // group, back, 0)
 
 
-def last_field(inputs, done, place, targets, sources, coefs, far_coupling, leaf_transfer, leaf_basis, upper_transfer, upper_coupling):
+def last_field(inputs, done, place, slots_of, levels, coefs, far_coupling, leaf_transfer, leaf_basis, upper_transfer, upper_coupling):
     leaves, leaf_size, rank = leaf_basis.shape
     columns, points = inputs[3].shape
     slots = inputs[1].shape[1]
@@ -371,37 +363,37 @@
     streamed = (coefs, far_coupling, leaf_transfer, leaf_basis, upper_transfer, upper_coupling)
     return pl.pallas_call(
         functools.partial(last_kernel, lo=lo, leaf_size=leaf_size),
-        in_specs=near_specs() + [vmem, smem, smem, smem] + [hbm] * len(streamed),
+        in_specs=near_specs() + [vmem, smem, smem, vmem, vmem, vmem] + [hbm] * len(streamed),
         out_specs=vmem,
         out_shape=jax.ShapeDtypeStruct((columns, points), F32),
         scratch_shapes=[pltpu.VMEM(x.shape, F32) for x in streamed]
         + [pltpu.VMEM((leaves + 1, columns, rank), F32), pltpu.SemaphoreType.DMA((len(streamed), 8))]
         + near_scratch(leaves - lo, slots, leaf_size),
-        compiler_params=pltpu.CompilerParams(vmem_limit_bytes=WIDE_LIMIT),
+        compiler_params=pltpu.CompilerParams(vmem_limit_bytes=LAST_LIMIT),
         cost_estimate=near_cost(leaves - lo, leaves, leaf_size),
-    )(*inputs, done, place, targets, sources, *streamed)
-
-
-def exchange(points, vectors, parts, width):
+    )(*inputs, done, place, slots_of, *levels, *streamed)
+
+
+def neighbours(points, vectors, width):
     axes = ("leaf", "top")
-    regions = lax.axis_size("leaf")
-    count = regions * lax.axis_size("top")
+    count = lax.axis_size("leaf") * lax.axis_size("top")
     head, tail = (jnp.concatenate([points[:, s], vectors[:, s]], axis=0) for s in (slice(0, width), slice(-width, None)))
+    before = lax.ppermute(tail, axes, [(i, i + 1) for i in range(count - 1)])
+    after = lax.ppermute(head, axes, [(i + 1, i) for i in range(count - 1)])
+    return (before[:3], before[3:]), (after[:3], after[3:])
+
+
+def siblings(sums):
+    count = lax.axis_size("leaf")
 
     def from_partner(x, distance):
-        return lax.ppermute(x, "leaf", [(i, i ^ distance) for i in range(regions)])
-
-    parts, head, tail = lax.optimization_barrier((parts, head, tail))
-    before = lax.ppermute(tail, axes, [(i, i + 1) for i in range(count - 1)])
-    other = from_partner(parts, 1)
-    before, other, head = lax.optimization_barrier((before, other, head))
-    level0, parts = other[0:1], parts[1:] + other[1:]
-    after = lax.ppermute(head, axes, [(i + 1, i) for i in range(count - 1)])
-    other = from_partner(parts, 2)
-    after, other = lax.optimization_barrier((after, other))
-    level1, parts = other[0:1], parts[1:] + other[1:]
-    level2 = from_partner(parts, 4)
-    return (before[:3], before[3:]), (after[:3], after[3:]), (level0, level1, level2)
+        return lax.ppermute(x, "leaf", [(i, i ^ distance) for i in range(count)])
+
+    other = from_partner(sums, 1)
+    level0, sums = other[0:1], sums[1:] + other[1:]
+    other = from_partner(sums, 2)
+    level1, sums = other[0:1], sums[1:] + other[1:]
+    return level0, level1, from_partner(sums, 4)
 
 
 def shards(
@@ -422,18 +414,19 @@
     place = region.astype(jnp.int32).reshape(1)
     first = ((region * peers + peer) * leaves).astype(jnp.int32).reshape(1)
 
-    coefs, parts = coefficients(place, vectors, leaf_basis, leaf_transfer, upper_transfer)
-    before, after, levels = exchange(points, vectors, parts, HALO * leaf_size)
-    coefs = lax.dynamic_update_slice_in_dim(coefs, jnp.concatenate(levels), leaves, 0)
+    coefs = coefficients(place, vectors, leaf_basis, leaf_transfer, upper_transfer)
     gathered = lax.all_gather(coefs, "top", axis=0)
+    before, after = neighbours(points, vectors, HALO * leaf_size)
     inputs = (first, near_offset, points, vectors, *before, *after)
     early = near_field(inputs, 0, EARLY_LEAVES)
+    gathered, early = lax.optimization_barrier((gathered, early))
+    levels = siblings(jnp.sum(gathered[:, leaves:], axis=0))
     return last_field(
         inputs,
         early,
         place,
-        far_target[0],
-        far_source[0],
+        jnp.concatenate([far_target[0], far_source[0]], axis=0),
+        levels,
         gathered,
         far_coupling[0],
         leaf_transfer,

time: 119 us -> 114 us (0.958)
  the two profiles are of different devices: /device:TPU:4 before, /device:TPU:2 now
where the time goes in v3:
time: 114 us; the launch traced here: 112 us
  Pallas kernels  73.8 us (65%)
  between operations  13.6 us (12%)
  starting transfers between devices  10.9 us (10%)
  waiting for transfers between devices  9.35 us (8%)
  local copies, waits for them, and re-layouts  2.81 us (2%)
  other arithmetic  1.64 us (1%)
    pallas_call x1, Pallas kernels, near_field(): pl.pallas_call(functools.partial(near_kernel, lo=lo, hi=hi, leaf_size=lea...  42.7 us
    pallas_call x1, Pallas kernels, last_field(): pl.pallas_call(functools.partial(last_kernel, lo=lo, leaf_size=leaf_size)...  23.7 us
    ppermute x3, waiting for transfers between devices, from_partner(): return lax.ppermute(x, 'leaf', [(i, i ^ distance) for i in range(count)])  7.59 us
    pallas_call x1, Pallas kernels, coefficients(): pl.pallas_call(functools.partial(coef_kernel, group=group), grid_spec=plt...  7.42 us
    ppermute x1, starting transfers between devices, neighbours(): after = lax.ppermute(head, axes, [(i + 1, i) for i in range(count - 1)])  6.3 us
    ppermute x1, starting transfers between devices, neighbours(): before = lax.ppermute(tail, axes, [(i, i + 1) for i in range(count - 1)])  3.48 us
  transfers between devices with their start and end apart: 6, of which 4 were waited for; matrix products, arithmetic and copies ran while one was open for 1% of the time, Pallas kernels for 38%

profile of v3, /device:TPU:2, one launch (start us, length us, event | category | flops | bytes accessed | tf_op | source)
XLA Modules:
  0.0 112.1 jit_solution(9909956822194157078)
XLA Ops:
  6.5 0.0 all-gather.3.cloned.1.call-start
  6.5 0.0 copy-start.2
  6.5 0.0 copy-start
  6.5 0.0 copy-start.11
  6.5 7.4 %shard_map.100 = f32[43,8,128]{2,1,0:T(8,128)} custom-call(s32[1]{0:T(128)} %bitcast.1.place_ref.refs_9_, f32[8,20480]{1,0:T(8,128)} %refs_3_.3, f32[40,512,128]{2,1,0:T(8,128)} %refs_17_.1, f32[40,128,128]{2,1,0:T(8,128)} %refs_16_.1, f32[12,128,128]{2,1,0:T(8,128)} %refs_18_.1, f32[12,128,128]{2,1,0:T(8,128)} %refs_18_.1), custom_call_target="tpu_custom_call" | custom-call | flops 209715200 | bytes 13107200 | tf_op jit(solution)/shard_map/pallas_call | solution.py:103
  14.0 0.0 all-gather.3.cloned.1.call-update
  14.0 0.0 copy-done.2
  14.0 0.0 copy-done
  14.1 3.5 %collective-permute-start = (f32[11,1024]{1,0:T(8,128)S(1)}, f32[11,1024]{1,0:T(8,128)S(1)}, u32[]{:S(2)}, u32[]{:S(2)}) collective-permute-start(f32[11,1024]{1,0:T(8,128)S(1)} %pad_maximum_fusion), channel_id=1, source_target_pairs={{0,1},{1,2},{2,3},{3,4},{4,5},{5,6},{6,7},{7,8},{8,9},{9,10},{10,1... | collective-permute-start | bytes 135176 | tf_op jit(solution)/shard_map/ppermute | solution.py:381
  17.6 6.3 %collective-permute-start.1 = (f32[11,1024]{1,0:T(8,128)S(1)}, f32[11,1024]{1,0:T(8,128)S(1)}, u32[]{:S(2)}, u32[]{:S(2)}) collective-permute-start(f32[11,1024]{1,0:T(8,128)S(1)} %pad_maximum_fusion.1), channel_id=1, source_target_pairs={{1,0},{2,1},{3,2},{4,3},{5,4},{6,5},{7,6},{8,7},{9,8},{10,9},{11,1... | collective-permute-start | bytes 135176 | tf_op jit(solution)/shard_map/ppermute | solution.py:382
  23.9 0.0 copy-done.11
  23.9 0.1 copy.16.refs_1_
  24.0 0.0 copy-start.5
  24.0 0.0 collective-permute-done
  24.0 0.0 copy-start.6
  24.0 0.0 copy-start.3
  24.0 1.7 %collective-permute-done.1 = f32[11,1024]{1,0:T(8,128)S(1)} collective-permute-done((f32[11,1024]{1,0:T(8,128)S(1)}, f32[11,1024]{1,0:T(8,128)S(1)}, u32[]{:S(2)}, u32[]{:S(2)}) %collective-permute-start.1) | collective-permute-done | bytes 45088 | tf_op jit(solution)/shard_map/ppermute | solution.py:382
  25.8 0.0 copy-start.7
  25.8 0.0 copy-start.4
  25.8 0.0 copy-start.8
  25.8 0.0 copy-start.9
  25.8 42.7 %shard_map.101.refs_8_ = f32[8,16384]{1,0:T(8,128)S(1)} custom-call(s32[1]{0:T(128)} %bitcast.refs_0_, s32[40,2]{1,0:T(8,128)S(1)} %copy.16.refs_1_, f32[3,20480]{1,0:T(4,128)S(1)} %copy-done.2, f32[8,20480]{1,0:T(8,128)S(1)} %copy-done, f32[3,1024]{1,0:T(4,128)S(1)} %slice.60.refs_4_, f32[8,1024]{1,0:T(8,128)S(1)} %slice.61.refs_5_, ...), custom_call_target="tpu_custom_call" | custom-call | flops 12884901888 | bytes 1802240 | tf_op jit(solution)/shard_map/pallas_call | solution.py:293
  68.5 0.0 copy-done.5
  68.5 0.0 copy-done.6
  68.5 0.0 copy-done.3
  68.5 0.0 copy-done.7
  68.6 0.0 copy-done.4
  68.6 0.0 copy-start.1
  68.6 0.8 copy-done.1
  69.4 0.0 all-gather.3.cloned.1.call-done
  69.4 1.0 slice_reduce_fusion
  70.3 0.2 collective-permute-start.2
  70.5 1.1 collective-permute-done.2
  71.6 0.0 collective-permute-start.3
  71.6 3.6 %collective-permute-done.3 = f32[2,8,128]{2,1,0:T(8,128)S(1)} collective-permute-done((f32[2,8,128]{2,1,0:T(8,128)S(1)}, f32[2,8,128]{2,1,0:T(8,128)S(1)}, u32[]{:S(2)}, u32[]{:S(2)}) %collective-permute-start.3) | collective-permute-done | bytes 8224 | tf_op jit(solution)/shard_map/ppermute | solution.py:390
  75.2 0.6 slice_add_fusion.1
  75.8 0.9 collective-permute-start.4
  76.7 0.0 copy-done.8
  76.7 0.0 copy-done.9
  76.7 0.1 pad_add_fusion
  76.8 0.7 copy.17.refs_10_
  77.5 0.6 slice.64.refs_11_
  78.1 2.8 %collective-permute-done.4.refs_13_ = f32[1,8,128]{2,1,0:T(8,128)S(1)} collective-permute-done((f32[1,8,128]{2,1,0:T(8,128)S(1)}, f32[1,8,128]{2,1,0:T(8,128)S(1)}, u32[]{:S(2)}, u32[]{:S(2)}) %collective-permute-start.4) | collective-permute-done | bytes 4128 | tf_op jit(solution)/shard_map/ppermute | solution.py:390
  80.9 0.0 copy-start.10
  80.9 0.6 copy-done.10
  81.5 23.7 %shard_map.102 = f32[8,20480]{1,0:T(8,128)} custom-call(s32[1]{0:T(128)} %bitcast.refs_0_, s32[40,2]{1,0:T(8,128)} %copy-done.5, f32[3,20480]{1,0:T(4,128)} %refs_2_.3, f32[8,20480]{1,0:T(8,128)} %refs_3_.3, f32[3,1024]{1,0:T(4,128)} %copy-done.6, f32[8,1024]{1,0:T(8,128)} %copy-done.3, f32[3,1024]{1,0:T(4,128)} %copy-done.7, f32[8,1024]{1,0:T(8,128)} %copy-done.4, ...), custom_call_target="tpu_custom_call" | custom-call | flops 3221225472 | bytes 1802240 | tf_op jit(solution)/shard_map/pallas_call | solution.py:364
  (9 shorter events, 0.1 us)
Async XLA Ops:
  6.5 62.8 %all-gather.3.cloned.1.call-start = ((), (), s32[]{:S(2)}) async-start(), calls=%async_computation | async-start | bytes 2994176 | tf_op jit(solution)/shard_map/all_gather | solution.py:418
  6.5 7.5 %copy-start.2 = (f32[3,20480]{1,0:T(4,128)S(1)}, f32[3,20480]{1,0:T(4,128)}, u32[]{:S(2)}) copy-start(f32[3,20480]{1,0:T(4,128)} %refs_2_.3) | copy-start | bytes 737284
  6.5 7.5 %copy-start = (f32[8,20480]{1,0:T(8,128)S(1)}, f32[8,20480]{1,0:T(8,128)}, u32[]{:S(2)}) copy-start(f32[8,20480]{1,0:T(8,128)} %refs_3_.3) | copy-start | bytes 1966084
  6.5 17.3 %copy-start.11 = (s32[40,2]{0,1:T(2,128)S(1)}, s32[40,2]{0,1:T(2,128)}, u32[]{:S(2)}) copy-start(s32[40,2]{0,1:T(2,128)} %param.12) | copy-start | bytes 964
  14.1 9.9 %collective-permute-start = (f32[11,1024]{1,0:T(8,128)S(1)}, f32[11,1024]{1,0:T(8,128)S(1)}, u32[]{:S(2)}, u32[]{:S(2)}) collective-permute-start(f32[11,1024]{1,0:T(8,128)S(1)} %pad_maximum_fusion), channel_id=1, source_target_pairs={{0,1},{1,2},{2,3},{3,4},{4,5},{5,6},{6,7},{7,8},{8,9},{9,10},{10,1... | collective-permute-start | bytes 135176 | tf_op jit(solution)/shard_map/ppermute | solution.py:381
  17.6 8.2 %collective-permute-start.1 = (f32[11,1024]{1,0:T(8,128)S(1)}, f32[11,1024]{1,0:T(8,128)S(1)}, u32[]{:S(2)}, u32[]{:S(2)}) collective-permute-start(f32[11,1024]{1,0:T(8,128)S(1)} %pad_maximum_fusion.1), channel_id=1, source_target_pairs={{1,0},{2,1},{3,2},{4,3},{5,4},{6,5},{7,6},{8,7},{9,8},{10,9},{11,1... | collective-permute-start | bytes 135176 | tf_op jit(solution)/shard_map/ppermute | solution.py:382
  24.0 44.5 %copy-start.5 = (s32[40,2]{1,0:T(8,128)}, s32[40,2]{1,0:T(8,128)S(1)}, u32[]{:S(2)}) copy-start(s32[40,2]{1,0:T(8,128)S(1)} %copy.16.refs_1_) | copy-start | bytes 964
  24.0 44.5 %copy-start.6 = (f32[3,1024]{1,0:T(4,128)}, f32[3,1024]{1,0:T(4,128)S(1)}, u32[]{:S(2)}) copy-start(f32[3,1024]{1,0:T(4,128)S(1)} %slice.60.refs_4_) | copy-start | bytes 36868
  24.0 44.5 %copy-start.3 = (f32[8,1024]{1,0:T(8,128)}, f32[8,1024]{1,0:T(8,128)S(1)}, u32[]{:S(2)}) copy-start(f32[8,1024]{1,0:T(8,128)S(1)} %slice.61.refs_5_) | copy-start | bytes 98308
  25.8 42.8 %copy-start.7 = (f32[3,1024]{1,0:T(4,128)}, f32[3,1024]{1,0:T(4,128)S(1)}, u32[]{:S(2)}) copy-start(f32[3,1024]{1,0:T(4,128)S(1)} %slice.62.refs_6_) | copy-start | bytes 36868
  25.8 42.8 %copy-start.4 = (f32[8,1024]{1,0:T(8,128)}, f32[8,1024]{1,0:T(8,128)S(1)}, u32[]{:S(2)}) copy-start(f32[8,1024]{1,0:T(8,128)S(1)} %slice.63.refs_7_) | copy-start | bytes 98308
  25.8 51.0 %copy-start.8 = (s32[1,16,8]{1,2,0:T(8,128)S(1)}, s32[1,16,8]{1,2,0:T(8,128)}, u32[]{:S(2)}) copy-start(s32[1,16,8]{1,2,0:T(8,128)} %param.16) | copy-start | bytes 1540
  25.8 50.9 %copy-start.9 = (s32[1,16,8]{1,2,0:T(8,128)S(1)}, s32[1,16,8]{1,2,0:T(8,128)}, u32[]{:S(2)}) copy-start(s32[1,16,8]{1,2,0:T(8,128)} %param.15) | copy-start | bytes 1540
  68.6 0.8 copy-start.1
  70.3 1.3 %collective-permute-start.2 = (f32[3,8,128]{2,1,0:T(8,128)S(1)}, f32[3,8,128]{2,1,0:T(8,128)S(1)}, u32[]{:S(2)}, u32[]{:S(2)}) collective-permute-start(f32[3,8,128]{2,1,0:T(8,128)S(1)} %slice_reduce_fusion), channel_id=1, source_target_pairs={{0,16},{16,0},{32,48},{48,32},{64,80},{80,64},{96,112},{112,96},{1... | collective-permute-start | bytes 36872 | tf_op jit(solution)/shard_map/ppermute | solution.py:390
  71.6 3.7 %collective-permute-start.3 = (f32[2,8,128]{2,1,0:T(8,128)S(1)}, f32[2,8,128]{2,1,0:T(8,128)S(1)}, u32[]{:S(2)}, u32[]{:S(2)}) collective-permute-start(f32[2,8,128]{2,1,0:T(8,128)S(1)} %slice_add_fusion), channel_id=1, source_target_pairs={{0,32},{16,48},{32,0},{48,16},{64,96},{80,112},{96,64},{112,80},{1... | collective-permute-start | bytes 24584 | tf_op jit(solution)/shard_map/ppermute | solution.py:390
  75.8 5.1 %collective-permute-start.4 = (f32[1,8,128]{2,1,0:T(8,128)S(1)}, f32[1,8,128]{2,1,0:T(8,128)S(1)}, u32[]{:S(2)}, u32[]{:S(2)}) collective-permute-start(f32[1,8,128]{2,1,0:T(8,128)S(1)} %get-tuple-element.13), channel_id=1, source_target_pairs={{0,64},{16,80},{32,96},{48,112},{64,0},{80,16},{96,32},{112,48},{1... | collective-permute-start | bytes 12296 | tf_op jit(solution)/shard_map/ppermute | solution.py:390
  80.9 0.6 copy-start.10
Sparse Core Ops, SparseCore 0:
  14.1 49.4 all-gather.2

commit v4 on v3

--- a/solution.py
+++ b/solution.py
@@ -160,7 +160,7 @@
 def near_core(inputs, out_ref, scratch, *, lo, hi, base, leaf_size):
     first_ref, offset_ref, points_ref, vectors_ref, before_p, before_v, after_p, after_v = inputs
     wide_scr, x_scr, a_scr, v_scr, b0, b1, u_scr, kh_scr, kl_scr, item_g, item_h = scratch
-    leaves = offset_ref.shape[0]
+    slots, leaves = offset_ref.shape
     first = first_ref[0]
     row8 = lax.broadcasted_iota(jnp.int32, (8, leaf_size), 0)
 
@@ -197,8 +197,8 @@
         item_g[n] = g - lo
         item_h[n] = g - lo + HALO
         n = n + 1
-        for j in range(offset_ref.shape[1]):
-            offset = offset_ref[g, j]
+        for j in range(slots):
+            offset = offset_ref[j, g]
             item_g[n] = g - lo
             item_h[n] = g - lo + HALO + offset
             n = n + jnp.where(offset != 0, 1, 0)
@@ -287,7 +287,7 @@
 
 
 def near_field(inputs, lo, hi):
-    leaves, slots = inputs[1].shape
+    slots, leaves = inputs[1].shape
     columns, points = inputs[3].shape
     leaf_size = points // leaves
     return pl.pallas_call(
@@ -303,8 +303,8 @@
 
 def last_kernel(*refs, lo, leaf_size):
     inputs = refs[:NEAR_INPUTS]
-    done_ref, place_ref, slot_ref, level0, level1, level2, *hbm, out_ref = refs[NEAR_INPUTS : NEAR_INPUTS + 13]
-    coef, coupling, transfer, basis, down, across, local_scr, sems, *scratch = refs[NEAR_INPUTS + 13 :]
+    done_ref, place_ref, target_ref, source_ref, level0, level1, level2, *hbm, out_ref = refs[NEAR_INPUTS : NEAR_INPUTS + 14]
+    coef, coupling, transfer, basis, down, across, local_scr, sems, *scratch = refs[NEAR_INPUTS + 14 :]
     held = (coef, coupling, transfer, basis, down, across)
     peers, slots, _, _ = coupling.shape
     leaves = basis.shape[0]
@@ -329,14 +329,14 @@
         copy.wait()
 
     here = place_ref[0]
-    region = dot_plain(level2[0], across[12 + (here >> 2)])
-    region = dot_plain(level1[0], across[8 + (here >> 1)]) + dot_turned(region, down[8 + (here >> 1)])
+    region = dot_plain(level2[2], across[12 + (here >> 2)])
+    region = dot_plain(level1[1], across[8 + (here >> 1)]) + dot_turned(region, down[8 + (here >> 1)])
     region = dot_plain(level0[0], across[here]) + dot_turned(region, down[here])
 
     def far(p, _):
-        products = [dot_plain(coef[p, slot_ref[peers + p, k]], coupling[p, k]) for k in range(slots)]
+        products = [dot_plain(coef[p, source_ref[k, p]], coupling[p, k]) for k in range(slots)]
         for k in range(slots):
-            local_scr[slot_ref[p, k]] += products[k]
+            local_scr[target_ref[k, p]] += products[k]
         return 0
 
     lax.fori_loop(0, peers, far, 0)
@@ -353,17 +353,17 @@
     lax.fori_loop(0, leaves // group, back, 0)
 
 
-def last_field(inputs, done, place, slots_of, levels, coefs, far_coupling, leaf_transfer, leaf_basis, upper_transfer, upper_coupling):
+def last_field(inputs, done, place, targets, sources, levels, coefs, far_coupling, leaf_transfer, leaf_basis, upper_transfer, upper_coupling):
     leaves, leaf_size, rank = leaf_basis.shape
     columns, points = inputs[3].shape
-    slots = inputs[1].shape[1]
+    slots = inputs[1].shape[0]
     lo = done.shape[1] // leaf_size
     smem, vmem = pl.BlockSpec(memory_space=pltpu.SMEM), pl.BlockSpec(memory_space=pltpu.VMEM)
     hbm = pl.BlockSpec(memory_space=pl.ANY)
     streamed = (coefs, far_coupling, leaf_transfer, leaf_basis, upper_transfer, upper_coupling)
     return pl.pallas_call(
         functools.partial(last_kernel, lo=lo, leaf_size=leaf_size),
-        in_specs=near_specs() + [vmem, smem, smem, vmem, vmem, vmem] + [hbm] * len(streamed),
+        in_specs=near_specs() + [vmem, smem, smem, smem, vmem, vmem, vmem] + [hbm] * len(streamed),
         out_specs=vmem,
         out_shape=jax.ShapeDtypeStruct((columns, points), F32),
         scratch_shapes=[pltpu.VMEM(x.shape, F32) for x in streamed]
@@ -371,7 +371,7 @@
         + near_scratch(leaves - lo, slots, leaf_size),
         compiler_params=pltpu.CompilerParams(vmem_limit_bytes=LAST_LIMIT),
         cost_estimate=near_cost(leaves - lo, leaves, leaf_size),
-    )(*inputs, done, place, slots_of, *levels, *streamed)
+    )(*inputs, done, place, targets, sources, *levels, *streamed)
 
 
 def neighbours(points, vectors, width):
@@ -389,11 +389,9 @@
     def from_partner(x, distance):
         return lax.ppermute(x, "leaf", [(i, i ^ distance) for i in range(count)])
 
-    other = from_partner(sums, 1)
-    level0, sums = other[0:1], sums[1:] + other[1:]
-    other = from_partner(sums, 2)
-    level1, sums = other[0:1], sums[1:] + other[1:]
-    return level0, level1, from_partner(sums, 4)
+    first = from_partner(sums, 1)
+    second = from_partner(sums + first, 2)
+    return first, second, from_partner(sums + first + second, 4)
 
 
 def shards(
@@ -417,7 +415,7 @@
     coefs = coefficients(place, vectors, leaf_basis, leaf_transfer, upper_transfer)
     gathered = lax.all_gather(coefs, "top", axis=0)
     before, after = neighbours(points, vectors, HALO * leaf_size)
-    inputs = (first, near_offset, points, vectors, *before, *after)
+    inputs = (first, near_offset.T, points, vectors, *before, *after)
     early = near_field(inputs, 0, EARLY_LEAVES)
     gathered, early = lax.optimization_barrier((gathered, early))
     levels = siblings(jnp.sum(gathered[:, leaves:], axis=0))
@@ -425,7 +423,8 @@
         inputs,
         early,
         place,
-        jnp.concatenate([far_target[0], far_source[0]], axis=0),
+        far_target[0].T,
+        far_source[0].T,
         levels,
         gathered,
         far_coupling[0],

time: 114 us -> 113 us (level)
  starting transfers between devices: 10.9 us -> 13.7 us
  local copies, waits for them, and re-layouts: 2.81 us -> 1.44 us
  waiting for transfers between devices: 9.35 us -> 8.1 us
    ppermute x3, starting transfers between devices: 1.07 us -> 3.96 us  [from_partner(): return lax.ppermute(x, 'leaf', [(i, i ^ distance) for i in range(count)])]
    ppermute x3, waiting for transfers between devices: 7.59 us -> 6.26 us  [from_partner(): return lax.ppermute(x, 'leaf', [(i, i ^ distance) for i in range(count)])]
  transfers between devices with their start and end apart: 6 -> 6, of which waited for: 4 -> 4; matrix products, arithmetic and copies ran while one was open for 1% -> 0% of each run, Pallas kernels for 38% -> 38%
where the time goes in v4:
time: 113 us; the launch traced here: 111 us
  Pallas kernels  73.5 us (65%)
  starting transfers between devices  13.7 us (12%)
  between operations  13.6 us (12%)
  waiting for transfers between devices  8.1 us (7%)
  local copies, waits for them, and re-layouts  1.44 us (1%)
    pallas_call x1, Pallas kernels, near_field(): pl.pallas_call(functools.partial(near_kernel, lo=lo, hi=hi, leaf_size=lea...  42.4 us
    pallas_call x1, Pallas kernels, last_field(): pl.pallas_call(functools.partial(last_kernel, lo=lo, leaf_size=leaf_size)...  23.7 us
    pallas_call x1, Pallas kernels, coefficients(): pl.pallas_call(functools.partial(coef_kernel, group=group), grid_spec=plt...  7.42 us
    ppermute x1, starting transfers between devices, neighbours(): after = lax.ppermute(head, axes, [(i + 1, i) for i in range(count - 1)])  6.3 us
    ppermute x3, waiting for transfers between devices, from_partner(): return lax.ppermute(x, 'leaf', [(i, i ^ distance) for i in range(count)])  6.26 us
    ppermute x3, starting transfers between devices, from_partner(): return lax.ppermute(x, 'leaf', [(i, i ^ distance) for i in range(count)])  3.96 us
    ppermute x1, starting transfers between devices, neighbours(): before = lax.ppermute(tail, axes, [(i, i + 1) for i in range(count - 1)])  3.48 us
  transfers between devices with their start and end apart: 6, of which 4 were waited for; matrix products, arithmetic and copies ran while one was open for 0% of the time, Pallas kernels for 38%

profile of v4, /device:TPU:2, one launch (start us, length us, event | category | flops | bytes accessed | tf_op | source)
XLA Modules:
  0.0 111.4 jit_solution(2919166701389853136)
XLA Ops:
  6.5 0.0 all-gather.3.cloned.1.call-start
  6.5 0.0 copy-start.2
  6.5 0.0 copy-start
  6.5 0.0 copy-start.7
  6.5 7.4 %shard_map.100 = f32[43,8,128]{2,1,0:T(8,128)} custom-call(s32[1]{0:T(128)} %bitcast.2.place_ref.refs_9_, f32[8,20480]{1,0:T(8,128)} %refs_3_.3, f32[40,512,128]{2,1,0:T(8,128)} %refs_18_.1, f32[40,128,128]{2,1,0:T(8,128)} %refs_17_.1, f32[12,128,128]{2,1,0:T(8,128)} %refs_19_.1, f32[12,128,128]{2,1,0:T(8,128)} %refs_19_.1), custom_call_target="tpu_custom_call" | custom-call | flops 209715200 | bytes 13107200 | tf_op jit(solution)/shard_map/pallas_call | solution.py:103
  14.0 0.0 all-gather.3.cloned.1.call-update
  14.0 0.0 copy-done.2
  14.0 0.0 copy-done
  14.1 3.5 %collective-permute-start = (f32[11,1024]{1,0:T(8,128)S(1)}, f32[11,1024]{1,0:T(8,128)S(1)}, u32[]{:S(2)}, u32[]{:S(2)}) collective-permute-start(f32[11,1024]{1,0:T(8,128)S(1)} %pad_maximum_fusion), channel_id=1, source_target_pairs={{0,1},{1,2},{2,3},{3,4},{4,5},{5,6},{6,7},{7,8},{8,9},{9,10},{10,1... | collective-permute-start | bytes 135176 | tf_op jit(solution)/shard_map/ppermute | solution.py:381
  17.6 6.3 %collective-permute-start.1 = (f32[11,1024]{1,0:T(8,128)S(1)}, f32[11,1024]{1,0:T(8,128)S(1)}, u32[]{:S(2)}, u32[]{:S(2)}) collective-permute-start(f32[11,1024]{1,0:T(8,128)S(1)} %pad_maximum_fusion.1), channel_id=1, source_target_pairs={{1,0},{2,1},{3,2},{4,3},{5,4},{6,5},{7,6},{8,7},{9,8},{10,9},{11,1... | collective-permute-start | bytes 135176 | tf_op jit(solution)/shard_map/ppermute | solution.py:382
  23.9 0.0 collective-permute-done
  23.9 0.0 copy-start.5
  23.9 0.0 copy-start.3
  23.9 1.8 %collective-permute-done.1 = f32[11,1024]{1,0:T(8,128)S(1)} collective-permute-done((f32[11,1024]{1,0:T(8,128)S(1)}, f32[11,1024]{1,0:T(8,128)S(1)}, u32[]{:S(2)}, u32[]{:S(2)}) %collective-permute-start.1) | collective-permute-done | bytes 45088 | tf_op jit(solution)/shard_map/ppermute | solution.py:382
  25.8 0.0 copy-start.6
  25.8 0.0 copy-start.4
  25.8 0.0 copy-done.7
  25.8 42.4 %shard_map.101.refs_8_ = f32[8,16384]{1,0:T(8,128)S(1)} custom-call(s32[1]{0:T(128)} %bitcast.refs_0_, s32[2,40]{1,0:T(2,128)S(1)} %bitcast.12, f32[3,20480]{1,0:T(4,128)S(1)} %copy-done.2, f32[8,20480]{1,0:T(8,128)S(1)} %copy-done, f32[3,1024]{1,0:T(4,128)S(1)} %slice.36.refs_4_, f32[8,1024]{1,0:T(8,128)S(1)} %slice.37.refs_5_, ...), custom_call_target="tpu_custom_call" | custom-call | flops 12884901888 | bytes 1802240 | tf_op jit(solution)/shard_map/pallas_call | solution.py:293
  68.2 0.0 copy-done.5
  68.2 0.0 copy-done.3
  68.2 0.0 copy-done.6
  68.2 0.0 copy-done.4
  68.2 0.0 copy-start.1
  68.3 0.8 copy-done.1
  69.0 0.0 all-gather.3.cloned.1.call-done
  69.0 1.0 slice_reduce_fusion
  70.0 0.1 collective-permute-start.2
  70.1 1.2 %collective-permute-done.2.refs_12_ = f32[3,8,128]{2,1,0:T(8,128)S(1)} collective-permute-done((f32[3,8,128]{2,1,0:T(8,128)S(1)}, f32[3,8,128]{2,1,0:T(8,128)S(1)}, u32[]{:S(2)}, u32[]{:S(2)}) %collective-permute-start.2) | collective-permute-done | bytes 12320 | tf_op jit(solution)/shard_map/ppermute | solution.py:390
  71.3 0.0 copy-start.8
  71.3 0.3 collective-permute-start.3
  71.5 3.4 %collective-permute-done.3.refs_13_ = f32[3,8,128]{2,1,0:T(8,128)S(1)} collective-permute-done((f32[3,8,128]{2,1,0:T(8,128)S(1)}, f32[3,8,128]{2,1,0:T(8,128)S(1)}, u32[]{:S(2)}, u32[]{:S(2)}) %collective-permute-start.3) | collective-permute-done | bytes 12320 | tf_op jit(solution)/shard_map/ppermute | solution.py:390
  75.0 0.0 copy-start.9
  75.0 3.6 %collective-permute-start.4 = (f32[3,8,128]{2,1,0:T(8,128)S(1)}, f32[3,8,128]{2,1,0:T(8,128)S(1)}, u32[]{:S(2)}, u32[]{:S(2)}) collective-permute-start(f32[3,8,128]{2,1,0:T(8,128)S(1)} %add.12), channel_id=1, source_target_pairs={{0,64},{16,80},{32,96},{48,112},{64,0},{80,16},{96,32},{112,48},{1... | collective-permute-start | bytes 36872 | tf_op jit(solution)/shard_map/ppermute | solution.py:390
  78.6 1.7 %collective-permute-done.4.refs_14_ = f32[3,8,128]{2,1,0:T(8,128)S(1)} collective-permute-done((f32[3,8,128]{2,1,0:T(8,128)S(1)}, f32[3,8,128]{2,1,0:T(8,128)S(1)}, u32[]{:S(2)}, u32[]{:S(2)}) %collective-permute-start.4) | collective-permute-done | bytes 12320 | tf_op jit(solution)/shard_map/ppermute | solution.py:390
  80.2 0.0 copy-start.10
  80.2 0.0 copy-done.8
  80.2 0.0 copy-done.9
  80.2 0.6 copy-done.10
  80.8 23.7 %shard_map.102 = f32[8,20480]{1,0:T(8,128)} custom-call(s32[1]{0:T(128)} %bitcast.refs_0_, s32[2,40]{1,0:T(2,128)} %bitcast.11, f32[3,20480]{1,0:T(4,128)} %refs_2_.3, f32[8,20480]{1,0:T(8,128)} %refs_3_.3, f32[3,1024]{1,0:T(4,128)} %copy-done.5, f32[8,1024]{1,0:T(8,128)} %copy-done.3, f32[3,1024]{1,0:T(4,128)} %copy-done.6, f32[8,1024]{1,0:T(8,128)} %copy-done.4, ...), custom_call_target="tpu_custom_call" | custom-call | flops 3221225472 | bytes 1802240 | tf_op jit(solution)/shard_map/pallas_call | solution.py:364
  (10 shorter events, 0.1 us)
Async XLA Ops:
  6.5 62.5 %all-gather.3.cloned.1.call-start = ((), (), s32[]{:S(2)}) async-start(), calls=%async_computation | async-start | bytes 2994176 | tf_op jit(solution)/shard_map/all_gather | solution.py:416
  6.5 7.5 %copy-start.2 = (f32[3,20480]{1,0:T(4,128)S(1)}, f32[3,20480]{1,0:T(4,128)}, u32[]{:S(2)}) copy-start(f32[3,20480]{1,0:T(4,128)} %refs_2_.3) | copy-start | bytes 737284
  6.5 7.5 %copy-start = (f32[8,20480]{1,0:T(8,128)S(1)}, f32[8,20480]{1,0:T(8,128)}, u32[]{:S(2)}) copy-start(f32[8,20480]{1,0:T(8,128)} %refs_3_.3) | copy-start | bytes 1966084
  6.5 19.3 %copy-start.7 = (s32[40,2]{0,1:T(2,128)S(1)}, s32[40,2]{0,1:T(2,128)}, u32[]{:S(2)}) copy-start(s32[40,2]{0,1:T(2,128)} %param.12) | copy-start | bytes 964
  14.1 9.8 %collective-permute-start = (f32[11,1024]{1,0:T(8,128)S(1)}, f32[11,1024]{1,0:T(8,128)S(1)}, u32[]{:S(2)}, u32[]{:S(2)}) collective-permute-start(f32[11,1024]{1,0:T(8,128)S(1)} %pad_maximum_fusion), channel_id=1, source_target_pairs={{0,1},{1,2},{2,3},{3,4},{4,5},{5,6},{6,7},{7,8},{8,9},{9,10},{10,1... | collective-permute-start | bytes 135176 | tf_op jit(solution)/shard_map/ppermute | solution.py:381
  17.6 8.2 %collective-permute-start.1 = (f32[11,1024]{1,0:T(8,128)S(1)}, f32[11,1024]{1,0:T(8,128)S(1)}, u32[]{:S(2)}, u32[]{:S(2)}) collective-permute-start(f32[11,1024]{1,0:T(8,128)S(1)} %pad_maximum_fusion.1), channel_id=1, source_target_pairs={{1,0},{2,1},{3,2},{4,3},{5,4},{6,5},{7,6},{8,7},{9,8},{10,9},{11,1... | collective-permute-start | bytes 135176 | tf_op jit(solution)/shard_map/ppermute | solution.py:382
  23.9 44.3 %copy-start.5 = (f32[3,1024]{1,0:T(4,128)}, f32[3,1024]{1,0:T(4,128)S(1)}, u32[]{:S(2)}) copy-start(f32[3,1024]{1,0:T(4,128)S(1)} %slice.36.refs_4_) | copy-start | bytes 36868
  23.9 44.3 %copy-start.3 = (f32[8,1024]{1,0:T(8,128)}, f32[8,1024]{1,0:T(8,128)S(1)}, u32[]{:S(2)}) copy-start(f32[8,1024]{1,0:T(8,128)S(1)} %slice.37.refs_5_) | copy-start | bytes 98308
  25.8 42.5 %copy-start.6 = (f32[3,1024]{1,0:T(4,128)}, f32[3,1024]{1,0:T(4,128)S(1)}, u32[]{:S(2)}) copy-start(f32[3,1024]{1,0:T(4,128)S(1)} %slice.38.refs_6_) | copy-start | bytes 36868
  25.8 42.5 %copy-start.4 = (f32[8,1024]{1,0:T(8,128)}, f32[8,1024]{1,0:T(8,128)S(1)}, u32[]{:S(2)}) copy-start(f32[8,1024]{1,0:T(8,128)S(1)} %slice.39.refs_7_) | copy-start | bytes 98308
  68.2 0.8 copy-start.1
  70.0 1.3 %collective-permute-start.2 = (f32[3,8,128]{2,1,0:T(8,128)S(1)}, f32[3,8,128]{2,1,0:T(8,128)S(1)}, u32[]{:S(2)}, u32[]{:S(2)}) collective-permute-start(f32[3,8,128]{2,1,0:T(8,128)S(1)} %slice_reduce_fusion), channel_id=1, source_target_pairs={{0,16},{16,0},{32,48},{48,32},{64,80},{80,64},{96,112},{112,96},{1... | collective-permute-start | bytes 36872 | tf_op jit(solution)/shard_map/ppermute | solution.py:390
  71.3 9.0 %copy-start.8 = (f32[3,8,128]{2,1,0:T(8,128)}, f32[3,8,128]{2,1,0:T(8,128)S(1)}, u32[]{:S(2)}) copy-start(f32[3,8,128]{2,1,0:T(8,128)S(1)} %collective-permute-done.2.refs_12_) | copy-start | bytes 36868
  71.3 3.7 %collective-permute-start.3 = (f32[3,8,128]{2,1,0:T(8,128)S(1)}, f32[3,8,128]{2,1,0:T(8,128)S(1)}, u32[]{:S(2)}, u32[]{:S(2)}) collective-permute-start(f32[3,8,128]{2,1,0:T(8,128)S(1)} %add.11), channel_id=1, source_target_pairs={{0,32},{16,48},{32,0},{48,16},{64,96},{80,112},{96,64},{112,80},{1... | collective-permute-start | bytes 36872 | tf_op jit(solution)/shard_map/ppermute | solution.py:390
  75.0 5.3 %copy-start.9 = (f32[3,8,128]{2,1,0:T(8,128)}, f32[3,8,128]{2,1,0:T(8,128)S(1)}, u32[]{:S(2)}) copy-start(f32[3,8,128]{2,1,0:T(8,128)S(1)} %collective-permute-done.3.refs_13_) | copy-start | bytes 36868
  75.0 5.3 %collective-permute-start.4 = (f32[3,8,128]{2,1,0:T(8,128)S(1)}, f32[3,8,128]{2,1,0:T(8,128)S(1)}, u32[]{:S(2)}, u32[]{:S(2)}) collective-permute-start(f32[3,8,128]{2,1,0:T(8,128)S(1)} %add.12), channel_id=1, source_target_pairs={{0,64},{16,80},{32,96},{48,112},{64,0},{80,16},{96,32},{112,48},{1... | collective-permute-start | bytes 36872 | tf_op jit(solution)/shard_map/ppermute | solution.py:390
  80.2 0.6 copy-start.10
Sparse Core Ops, SparseCore 0:
  14.1 49.4 all-gather.2

commit v5 on v4

--- a/solution.py
+++ b/solution.py
@@ -22,7 +22,6 @@
 NEAR_LIMIT = 20 << 20
 WIDE_LIMIT = 56 << 20
 LAST_LIMIT = 56 << 20
-EARLY_LEAVES = 32
 
 
 def halves(x):
@@ -133,21 +132,15 @@
 def features(x, target):
     row = lax.broadcasted_iota(jnp.int32, x.shape, 0)
     norm = jnp.sum(x * x, axis=0, keepdims=True)
-    high, middle, low = thirds(jnp.where(row < 3, x, norm))
-    norm_row, one_row, factor = (4, 3, -2.0) if target else (3, 4, 1.0)
-
-    def group(coordinates, norms):
-        out = jnp.where(row < 3, coordinates * factor, 0.0)
-        if norms is not None:
-            out = jnp.where(row == norm_row, norms, jnp.where(row == one_row, 1.0, out))
-        return out
-
     if target:
-        groups = [group(high, high), group(middle, middle), group(high, low)]
-        groups += [group(low, None), group(middle, None), group(high, None)]
+        high, middle, low = thirds(jnp.where(row < 3, -2.0 * x, norm))
+        groups = [jnp.where(row == 3, 1.0, high), jnp.where(row == 3, 1.0, middle)]
+        groups += [jnp.where(row == 3, 1.0, jnp.where(row < 3, high, low)), low, middle, high]
     else:
-        groups = [group(high, high), group(middle, middle), group(low, low)]
-        groups += [group(high, None), group(high, None), group(middle, None)]
+        high, middle, low = thirds(jnp.where(row < 4, jnp.where(row < 3, x, norm), 0.0))
+        one = jnp.where(row == 4, 1.0, 0.0)
+        groups = [high + one, middle + one, low + one]
+        groups += [jnp.where(row < 3, high, 0.0), jnp.where(row < 3, high, 0.0), jnp.where(row < 3, middle, 0.0)]
     groups += [jnp.zeros_like(x)] * (DEPTH // 8 - 6)
     return jnp.concatenate(groups, axis=0)
 
@@ -157,7 +150,7 @@
     return nt * jnp.exp2(nt)
 
 
-def near_core(inputs, out_ref, scratch, *, lo, hi, base, leaf_size):
+def near_core(inputs, out_ref, scratch, *, begin, stop, leaf_size):
     first_ref, offset_ref, points_ref, vectors_ref, before_p, before_v, after_p, after_v = inputs
     wide_scr, x_scr, a_scr, v_scr, b0, b1, u_scr, kh_scr, kl_scr, item_g, item_h = scratch
     slots, leaves = offset_ref.shape
@@ -166,10 +159,26 @@
 
     wide_scr[...] = jnp.zeros_like(wide_scr)
 
+    def listing(g, n):
+        item_g[n] = g
+        item_h[n] = g + HALO
+        n = n + 1
+        for j in range(slots):
+            offset = offset_ref[j, g]
+            item_g[n] = g
+            item_h[n] = g + HALO + offset
+            n = n + jnp.where(offset != 0, 1, 0)
+        return n
+
+    count = lax.fori_loop(0, leaves, listing, 0)
+    end = count if stop is None else jnp.minimum(stop, count)
+    g_first = item_g[jnp.minimum(begin, count - 1)]
+    g_last = item_g[end - 1]
+
     def prepare(p_ref, v_ref, start, stop, origin):
         def turn(h, _):
             at = pl.ds(pl.multiple_of((h - origin) * leaf_size, leaf_size), leaf_size)
-            to = h + HALO - lo
+            to = h + HALO
             centre = (first + h).astype(F32) * 0.5 + 0.5
             wide_scr[0:3] = p_ref[:, at]
             shift = jnp.where(row8 == 0, centre, 0.5)
@@ -184,27 +193,9 @@
 
         lax.fori_loop(start, stop, turn, 0)
 
-    if lo < HALO:
-        prepare(before_p, before_v, -HALO, 0, -HALO)
-    prepare(points_ref, vectors_ref, max(lo - HALO, 0), min(hi + HALO, leaves), 0)
-    if hi > leaves - HALO:
-        prepare(after_p, after_v, leaves, leaves + HALO, leaves)
-
-    def listing(g, n):
-        at = pl.ds(pl.multiple_of(g * leaf_size, leaf_size), leaf_size)
-        to = pl.ds(pl.multiple_of((g - base) * leaf_size, leaf_size), leaf_size)
-        out_ref[:, to] = NUGGET * vectors_ref[:, at]
-        item_g[n] = g - lo
-        item_h[n] = g - lo + HALO
-        n = n + 1
-        for j in range(slots):
-            offset = offset_ref[j, g]
-            item_g[n] = g - lo
-            item_h[n] = g - lo + HALO + offset
-            n = n + jnp.where(offset != 0, 1, 0)
-        return n
-
-    count = lax.fori_loop(lo, hi, listing, 0)
+    prepare(before_p, before_v, jnp.minimum(g_first - HALO, 0), 0, -HALO)
+    prepare(points_ref, vectors_ref, jnp.maximum(g_first - HALO, 0), jnp.minimum(g_last + HALO + 1, leaves), 0)
+    prepare(after_p, after_v, leaves, jnp.maximum(g_last + HALO + 1, leaves), leaves)
 
     def target_features(i, b_scr):
         i = jnp.minimum(i, count - 1)
@@ -232,21 +223,21 @@
             acc += jnp.dot(v_scr[h, 0:16, c : c + size], kh_scr[c : c + size], preferred_element_type=F32)
             acc += jnp.dot(v_scr[h, 16:32, c : c + size], kl_scr[c : c + size], preferred_element_type=F32)
         target_features(i + 2, b_later)
-        done = jnp.where(i < count, (acc[0:8] + acc[8:16]) * GAIN, 0.0)
-        at = pl.ds(pl.multiple_of((item_g[now] + (lo - base)) * leaf_size, leaf_size), leaf_size)
+        done = jnp.where(i < end, (acc[0:8] + acc[8:16]) * GAIN, 0.0)
+        at = pl.ds(pl.multiple_of(item_g[now] * leaf_size, leaf_size), leaf_size)
         out_ref[:, at] += done
 
-    target_features(0, b0)
-    target_features(1, b1)
-    distances(0, b0, 0, leaf_size)
+    target_features(begin, b0)
+    target_features(begin + 1, b1)
+    distances(begin, b0, 0, leaf_size)
 
     def turns(i, _):
         for j in range(0, UNROLL, 2):
-            turn(UNROLL * i + j, b1, b0)
-            turn(UNROLL * i + j + 1, b0, b1)
+            turn(begin + UNROLL * i + j, b1, b0)
+            turn(begin + UNROLL * i + j + 1, b0, b1)
         return 0
 
-    lax.fori_loop(0, (count + (UNROLL - 1)) >> UNROLL.bit_length() - 1, turns, 0)
+    lax.fori_loop(0, jnp.maximum(end - begin + (UNROLL - 1), 0) >> UNROLL.bit_length() - 1, turns, 0)
 
 
 def near_scratch(count, slots, leaf_size):
@@ -270,15 +261,17 @@
 NEAR_INPUTS = 8
 
 
-def near_kernel(*refs, lo, hi, leaf_size):
-    near_core(refs[:NEAR_INPUTS], refs[NEAR_INPUTS], refs[NEAR_INPUTS + 1 :], lo=lo, hi=hi, base=lo, leaf_size=leaf_size)
-
-
-def near_cost(count, leaves, leaf_size):
+def near_kernel(*refs, stop, leaf_size):
+    inputs, out_ref = refs[:NEAR_INPUTS], refs[NEAR_INPUTS]
+    out_ref[...] = NUGGET * inputs[3][...]
+    near_core(inputs, out_ref, refs[NEAR_INPUTS + 1 :], begin=0, stop=stop, leaf_size=leaf_size)
+
+
+def near_cost(blocks, leaves, leaf_size):
     return pl.CostEstimate(
-        flops=count * 3 * leaf_size * leaf_size * 512,
+        flops=blocks * leaf_size * leaf_size * 512,
         bytes_accessed=8 * 11 * leaves * leaf_size,
-        transcendentals=count * 6 * leaf_size * leaf_size,
+        transcendentals=blocks * 2 * leaf_size * leaf_size,
     )
 
 
@@ -286,22 +279,22 @@
     return [pl.BlockSpec(memory_space=pltpu.SMEM)] * 2 + [pl.BlockSpec(memory_space=pltpu.VMEM)] * 6
 
 
-def near_field(inputs, lo, hi):
+def near_field(inputs, stop):
     slots, leaves = inputs[1].shape
     columns, points = inputs[3].shape
     leaf_size = points // leaves
     return pl.pallas_call(
-        functools.partial(near_kernel, lo=lo, hi=hi, leaf_size=leaf_size),
+        functools.partial(near_kernel, stop=stop, leaf_size=leaf_size),
         in_specs=near_specs(),
         out_specs=pl.BlockSpec(memory_space=pltpu.VMEM),
-        out_shape=jax.ShapeDtypeStruct((columns, (hi - lo) * leaf_size), F32),
-        scratch_shapes=near_scratch(hi - lo, slots, leaf_size),
+        out_shape=jax.ShapeDtypeStruct((columns, points), F32),
+        scratch_shapes=near_scratch(leaves, slots, leaf_size),
         compiler_params=pltpu.CompilerParams(vmem_limit_bytes=NEAR_LIMIT),
-        cost_estimate=near_cost(hi - lo, leaves, leaf_size),
+        cost_estimate=near_cost(stop, leaves, leaf_size),
     )(*inputs)
 
 
-def last_kernel(*refs, lo, leaf_size):
+def last_kernel(*refs, begin, leaf_size):
     inputs = refs[:NEAR_INPUTS]
     done_ref, place_ref, target_ref, source_ref, level0, level1, level2, *hbm, out_ref = refs[NEAR_INPUTS : NEAR_INPUTS + 14]
     coef, coupling, transfer, basis, down, across, local_scr, sems, *scratch = refs[NEAR_INPUTS + 14 :]
@@ -321,9 +314,9 @@
     for copy in copies():
         copy.start()
 
-    out_ref[:, 0 : lo * leaf_size] = done_ref[...]
+    out_ref[...] = done_ref[...]
     local_scr[...] = jnp.zeros_like(local_scr)
-    near_core(inputs, out_ref, scratch, lo=lo, hi=leaves, base=0, leaf_size=leaf_size)
+    near_core(inputs, out_ref, scratch, begin=begin, stop=None, leaf_size=leaf_size)
 
     for copy in copies():
         copy.wait()
@@ -353,24 +346,23 @@
     lax.fori_loop(0, leaves // group, back, 0)
 
 
-def last_field(inputs, done, place, targets, sources, levels, coefs, far_coupling, leaf_transfer, leaf_basis, upper_transfer, upper_coupling):
+def last_field(inputs, begin, done, place, targets, sources, levels, coefs, far_coupling, leaf_transfer, leaf_basis, upper_transfer, upper_coupling):
     leaves, leaf_size, rank = leaf_basis.shape
     columns, points = inputs[3].shape
     slots = inputs[1].shape[0]
-    lo = done.shape[1] // leaf_size
     smem, vmem = pl.BlockSpec(memory_space=pltpu.SMEM), pl.BlockSpec(memory_space=pltpu.VMEM)
     hbm = pl.BlockSpec(memory_space=pl.ANY)
     streamed = (coefs, far_coupling, leaf_transfer, leaf_basis, upper_transfer, upper_coupling)
     return pl.pallas_call(
-        functools.partial(last_kernel, lo=lo, leaf_size=leaf_size),
+        functools.partial(last_kernel, begin=begin, leaf_size=leaf_size),
         in_specs=near_specs() + [vmem, smem, smem, smem, vmem, vmem, vmem] + [hbm] * len(streamed),
         out_specs=vmem,
         out_shape=jax.ShapeDtypeStruct((columns, points), F32),
         scratch_shapes=[pltpu.VMEM(x.shape, F32) for x in streamed]
         + [pltpu.VMEM((leaves + 1, columns, rank), F32), pltpu.SemaphoreType.DMA((len(streamed), 8))]
-        + near_scratch(leaves - lo, slots, leaf_size),
+        + near_scratch(leaves, slots, leaf_size),
         compiler_params=pltpu.CompilerParams(vmem_limit_bytes=LAST_LIMIT),
-        cost_estimate=near_cost(leaves - lo, leaves, leaf_size),
+        cost_estimate=near_cost(leaves, leaves, leaf_size),
     )(*inputs, done, place, targets, sources, *levels, *streamed)
 
 
@@ -416,11 +408,13 @@
     gathered = lax.all_gather(coefs, "top", axis=0)
     before, after = neighbours(points, vectors, HALO * leaf_size)
     inputs = (first, near_offset.T, points, vectors, *before, *after)
-    early = near_field(inputs, 0, EARLY_LEAVES)
+    early_blocks = 2 * leaves
+    early = near_field(inputs, early_blocks)
     gathered, early = lax.optimization_barrier((gathered, early))
     levels = siblings(jnp.sum(gathered[:, leaves:], axis=0))
     return last_field(
         inputs,
+        early_blocks,
         early,
         place,
         far_target[0].T,

time: 113 us -> 111 us (0.982)
  Pallas kernels: 73.5 us -> 72.1 us
    pallas_call x2, Pallas kernels: 66.1 us -> 64.6 us  [the longest x1 40.5 us: near_field(): pl.pallas_call(functools.partial(near_kernel, stop=stop, leaf_size=leaf_s...]
  transfers between devices with their start and end apart: 6 -> 6, of which waited for: 4 -> 4; matrix products, arithmetic and copies ran while one was open for 0% -> 0% of each run, Pallas kernels for 38% -> 37%
where the time goes in v5:
time: 111 us; the launch traced here: 110 us
  Pallas kernels  72.1 us (65%)
  between operations  13.6 us (12%)
  starting transfers between devices  13.1 us (12%)
  waiting for transfers between devices  8.69 us (8%)
  local copies, waits for them, and re-layouts  1.5 us (1%)
    pallas_call x1, Pallas kernels, near_field(): pl.pallas_call(functools.partial(near_kernel, stop=stop, leaf_size=leaf_s...  40.5 us
    pallas_call x1, Pallas kernels, last_field(): pl.pallas_call(functools.partial(last_kernel, begin=begin, leaf_size=leaf...  24.2 us
    pallas_call x1, Pallas kernels, coefficients(): pl.pallas_call(functools.partial(coef_kernel, group=group), grid_spec=plt...  7.42 us
    ppermute x3, waiting for transfers between devices, from_partner(): return lax.ppermute(x, 'leaf', [(i, i ^ distance) for i in range(count)])  6.85 us
    ppermute x1, starting transfers between devices, neighbours(): after = lax.ppermute(head, axes, [(i + 1, i) for i in range(count - 1)])  6.3 us
    ppermute x1, starting transfers between devices, neighbours(): before = lax.ppermute(tail, axes, [(i, i + 1) for i in range(count - 1)])  3.48 us
    ppermute x3, starting transfers between devices, from_partner(): return lax.ppermute(x, 'leaf', [(i, i ^ distance) for i in range(count)])  3.3 us
  transfers between devices with their start and end apart: 6, of which 4 were waited for; matrix products, arithmetic and copies ran while one was open for 0% of the time, Pallas kernels for 37%

profile of v5, /device:TPU:2, one launch (start us, length us, event | category | flops | bytes accessed | tf_op | source)
XLA Modules:
  0.0 109.9 jit_solution(9093035799680649579)
XLA Ops:
  6.5 0.0 all-gather.3.cloned.1.call-start
  6.5 0.0 copy-start.5
  6.5 0.0 copy-start
  6.5 0.0 copy-start.6
  6.5 7.4 %shard_map.100 = f32[43,8,128]{2,1,0:T(8,128)} custom-call(s32[1]{0:T(128)} %bitcast.2.place_ref.refs_9_, f32[8,20480]{1,0:T(8,128)} %refs_3_.3, f32[40,512,128]{2,1,0:T(8,128)} %refs_18_.1, f32[40,128,128]{2,1,0:T(8,128)} %refs_17_.1, f32[12,128,128]{2,1,0:T(8,128)} %refs_19_.1, f32[12,128,128]{2,1,0:T(8,128)} %refs_19_.1), custom_call_target="tpu_custom_call" | custom-call | flops 209715200 | bytes 13107200 | tf_op jit(solution)/shard_map/pallas_call | solution.py:102
  14.0 0.0 all-gather.3.cloned.1.call-update
  14.0 0.0 copy-done.5
  14.0 0.0 copy-done
  14.1 3.5 %collective-permute-start = (f32[11,1024]{1,0:T(8,128)S(1)}, f32[11,1024]{1,0:T(8,128)S(1)}, u32[]{:S(2)}, u32[]{:S(2)}) collective-permute-start(f32[11,1024]{1,0:T(8,128)S(1)} %pad_maximum_fusion), channel_id=1, source_target_pairs={{0,1},{1,2},{2,3},{3,4},{4,5},{5,6},{6,7},{7,8},{8,9},{9,10},{10,1... | collective-permute-start | bytes 135176 | tf_op jit(solution)/shard_map/ppermute | solution.py:373
  17.6 6.3 %collective-permute-start.1 = (f32[11,1024]{1,0:T(8,128)S(1)}, f32[11,1024]{1,0:T(8,128)S(1)}, u32[]{:S(2)}, u32[]{:S(2)}) collective-permute-start(f32[11,1024]{1,0:T(8,128)S(1)} %pad_maximum_fusion.1), channel_id=1, source_target_pairs={{1,0},{2,1},{3,2},{4,3},{5,4},{6,5},{7,6},{8,7},{9,8},{10,9},{11,1... | collective-permute-start | bytes 135176 | tf_op jit(solution)/shard_map/ppermute | solution.py:374
  23.9 0.0 collective-permute-done
  23.9 0.0 copy-start.3
  23.9 0.0 copy-start.1
  23.9 1.8 %collective-permute-done.1 = f32[11,1024]{1,0:T(8,128)S(1)} collective-permute-done((f32[11,1024]{1,0:T(8,128)S(1)}, f32[11,1024]{1,0:T(8,128)S(1)}, u32[]{:S(2)}, u32[]{:S(2)}) %collective-permute-start.1) | collective-permute-done | bytes 45088 | tf_op jit(solution)/shard_map/ppermute | solution.py:374
  25.8 0.0 copy-start.4
  25.8 0.0 copy-start.2
  25.8 0.0 copy-done.6
  25.8 40.5 %shard_map.101.refs_8_ = f32[8,20480]{1,0:T(8,128)S(1)} custom-call(s32[1]{0:T(128)} %bitcast.refs_0_, s32[2,40]{1,0:T(2,128)S(1)} %bitcast.12, f32[3,20480]{1,0:T(4,128)S(1)} %copy-done.5, f32[8,20480]{1,0:T(8,128)S(1)} %copy-done, f32[3,1024]{1,0:T(4,128)S(1)} %slice.36.refs_4_, f32[8,1024]{1,0:T(8,128)S(1)} %slice.37.refs_5_, ...), custom_call_target="tpu_custom_call" | custom-call | flops 10737418240 | bytes 1802240 | tf_op jit(solution)/shard_map/pallas_call | solution.py:286
  66.3 0.0 copy-done.3
  66.3 0.0 copy-done.1
  66.3 0.0 copy-done.4
  66.3 0.0 copy-done.2
  66.3 0.0 copy-start.7
  66.3 0.8 copy-done.7
  67.2 0.0 all-gather.3.cloned.1.call-done
  67.2 1.0 slice_reduce_fusion
  68.1 0.3 collective-permute-start.2
  68.4 1.0 collective-permute-done.2.refs_12_
  69.4 0.0 copy-start.8
  69.4 0.5 collective-permute-start.3
  69.9 3.2 %collective-permute-done.3.refs_13_ = f32[3,8,128]{2,1,0:T(8,128)S(1)} collective-permute-done((f32[3,8,128]{2,1,0:T(8,128)S(1)}, f32[3,8,128]{2,1,0:T(8,128)S(1)}, u32[]{:S(2)}, u32[]{:S(2)}) %collective-permute-start.3) | collective-permute-done | bytes 12320 | tf_op jit(solution)/shard_map/ppermute | solution.py:382
  73.1 0.0 copy-start.9
  73.1 2.5 %collective-permute-start.4 = (f32[3,8,128]{2,1,0:T(8,128)S(1)}, f32[3,8,128]{2,1,0:T(8,128)S(1)}, u32[]{:S(2)}, u32[]{:S(2)}) collective-permute-start(f32[3,8,128]{2,1,0:T(8,128)S(1)} %add.12), channel_id=1, source_target_pairs={{0,64},{16,80},{32,96},{48,112},{64,0},{80,16},{96,32},{112,48},{1... | collective-permute-start | bytes 36872 | tf_op jit(solution)/shard_map/ppermute | solution.py:382
  75.6 2.7 %collective-permute-done.4.refs_14_ = f32[3,8,128]{2,1,0:T(8,128)S(1)} collective-permute-done((f32[3,8,128]{2,1,0:T(8,128)S(1)}, f32[3,8,128]{2,1,0:T(8,128)S(1)}, u32[]{:S(2)}, u32[]{:S(2)}) %collective-permute-start.4) | collective-permute-done | bytes 12320 | tf_op jit(solution)/shard_map/ppermute | solution.py:382
  78.3 0.0 copy-start.10
  78.3 0.0 copy-done.8
  78.3 0.0 copy-done.9
  78.3 0.6 copy-done.10
  78.9 24.2 %shard_map.102 = f32[8,20480]{1,0:T(8,128)} custom-call(s32[1]{0:T(128)} %bitcast.refs_0_, s32[2,40]{1,0:T(2,128)} %bitcast.11, f32[3,20480]{1,0:T(4,128)} %refs_2_.3, f32[8,20480]{1,0:T(8,128)} %refs_3_.3, f32[3,1024]{1,0:T(4,128)} %copy-done.3, f32[8,1024]{1,0:T(8,128)} %copy-done.1, f32[3,1024]{1,0:T(4,128)} %copy-done.4, f32[8,1024]{1,0:T(8,128)} %copy-done.2, ...), custom_call_target="tpu_custom_call" | custom-call | flops 5368709120 | bytes 1802240 | tf_op jit(solution)/shard_map/pallas_call | solution.py:356
  (10 shorter events, 0.1 us)
Async XLA Ops:
  6.5 60.6 %all-gather.3.cloned.1.call-start = ((), (), s32[]{:S(2)}) async-start(), calls=%async_computation | async-start | bytes 2994176 | tf_op jit(solution)/shard_map/all_gather | solution.py:408
  6.5 7.5 %copy-start.5 = (f32[3,20480]{1,0:T(4,128)S(1)}, f32[3,20480]{1,0:T(4,128)}, u32[]{:S(2)}) copy-start(f32[3,20480]{1,0:T(4,128)} %refs_2_.3) | copy-start | bytes 737284
  6.5 7.5 %copy-start = (f32[8,20480]{1,0:T(8,128)S(1)}, f32[8,20480]{1,0:T(8,128)}, u32[]{:S(2)}) copy-start(f32[8,20480]{1,0:T(8,128)} %refs_3_.3) | copy-start | bytes 1966084
  6.5 19.3 %copy-start.6 = (s32[40,2]{0,1:T(2,128)S(1)}, s32[40,2]{0,1:T(2,128)}, u32[]{:S(2)}) copy-start(s32[40,2]{0,1:T(2,128)} %param.12) | copy-start | bytes 964
  14.1 9.8 %collective-permute-start = (f32[11,1024]{1,0:T(8,128)S(1)}, f32[11,1024]{1,0:T(8,128)S(1)}, u32[]{:S(2)}, u32[]{:S(2)}) collective-permute-start(f32[11,1024]{1,0:T(8,128)S(1)} %pad_maximum_fusion), channel_id=1, source_target_pairs={{0,1},{1,2},{2,3},{3,4},{4,5},{5,6},{6,7},{7,8},{8,9},{9,10},{10,1... | collective-permute-start | bytes 135176 | tf_op jit(solution)/shard_map/ppermute | solution.py:373
  17.6 8.2 %collective-permute-start.1 = (f32[11,1024]{1,0:T(8,128)S(1)}, f32[11,1024]{1,0:T(8,128)S(1)}, u32[]{:S(2)}, u32[]{:S(2)}) collective-permute-start(f32[11,1024]{1,0:T(8,128)S(1)} %pad_maximum_fusion.1), channel_id=1, source_target_pairs={{1,0},{2,1},{3,2},{4,3},{5,4},{6,5},{7,6},{8,7},{9,8},{10,9},{11,1... | collective-permute-start | bytes 135176 | tf_op jit(solution)/shard_map/ppermute | solution.py:374
  23.9 42.4 %copy-start.3 = (f32[3,1024]{1,0:T(4,128)}, f32[3,1024]{1,0:T(4,128)S(1)}, u32[]{:S(2)}) copy-start(f32[3,1024]{1,0:T(4,128)S(1)} %slice.36.refs_4_) | copy-start | bytes 36868
  23.9 42.4 %copy-start.1 = (f32[8,1024]{1,0:T(8,128)}, f32[8,1024]{1,0:T(8,128)S(1)}, u32[]{:S(2)}) copy-start(f32[8,1024]{1,0:T(8,128)S(1)} %slice.37.refs_5_) | copy-start | bytes 98308
  25.8 40.5 %copy-start.4 = (f32[3,1024]{1,0:T(4,128)}, f32[3,1024]{1,0:T(4,128)S(1)}, u32[]{:S(2)}) copy-start(f32[3,1024]{1,0:T(4,128)S(1)} %slice.38.refs_6_) | copy-start | bytes 36868
  25.8 40.5 %copy-start.2 = (f32[8,1024]{1,0:T(8,128)}, f32[8,1024]{1,0:T(8,128)S(1)}, u32[]{:S(2)}) copy-start(f32[8,1024]{1,0:T(8,128)S(1)} %slice.39.refs_7_) | copy-start | bytes 98308
  66.3 0.8 copy-start.7
  68.1 1.3 %collective-permute-start.2 = (f32[3,8,128]{2,1,0:T(8,128)S(1)}, f32[3,8,128]{2,1,0:T(8,128)S(1)}, u32[]{:S(2)}, u32[]{:S(2)}) collective-permute-start(f32[3,8,128]{2,1,0:T(8,128)S(1)} %slice_reduce_fusion), channel_id=1, source_target_pairs={{0,16},{16,0},{32,48},{48,32},{64,80},{80,64},{96,112},{112,96},{1... | collective-permute-start | bytes 36872 | tf_op jit(solution)/shard_map/ppermute | solution.py:382
  69.4 8.9 %copy-start.8 = (f32[3,8,128]{2,1,0:T(8,128)}, f32[3,8,128]{2,1,0:T(8,128)S(1)}, u32[]{:S(2)}) copy-start(f32[3,8,128]{2,1,0:T(8,128)S(1)} %collective-permute-done.2.refs_12_) | copy-start | bytes 36868
  69.4 3.7 %collective-permute-start.3 = (f32[3,8,128]{2,1,0:T(8,128)S(1)}, f32[3,8,128]{2,1,0:T(8,128)S(1)}, u32[]{:S(2)}, u32[]{:S(2)}) collective-permute-start(f32[3,8,128]{2,1,0:T(8,128)S(1)} %add.11), channel_id=1, source_target_pairs={{0,32},{16,48},{32,0},{48,16},{64,96},{80,112},{96,64},{112,80},{1... | collective-permute-start | bytes 36872 | tf_op jit(solution)/shard_map/ppermute | solution.py:382
  73.1 5.2 %copy-start.9 = (f32[3,8,128]{2,1,0:T(8,128)}, f32[3,8,128]{2,1,0:T(8,128)S(1)}, u32[]{:S(2)}) copy-start(f32[3,8,128]{2,1,0:T(8,128)S(1)} %collective-permute-done.3.refs_13_) | copy-start | bytes 36868
  73.1 5.2 %collective-permute-start.4 = (f32[3,8,128]{2,1,0:T(8,128)S(1)}, f32[3,8,128]{2,1,0:T(8,128)S(1)}, u32[]{:S(2)}, u32[]{:S(2)}) collective-permute-start(f32[3,8,128]{2,1,0:T(8,128)S(1)} %add.12), channel_id=1, source_target_pairs={{0,64},{16,80},{32,96},{48,112},{64,0},{80,16},{96,32},{112,48},{1... | collective-permute-start | bytes 36872 | tf_op jit(solution)/shard_map/ppermute | solution.py:382
  78.3 0.6 copy-start.10
Sparse Core Ops, SparseCore 0:
  14.1 49.4 all-gather.2

commit v6 on v5

--- a/solution.py
+++ b/solution.py
@@ -332,9 +332,9 @@
             local_scr[target_ref[k, p]] += products[k]
         return 0
 
-    lax.fori_loop(0, peers, far, 0)
-
-    group = 4
+    lax.fori_loop(0, peers, far, 0, unroll=2)
+
+    group = 8
 
     def back(i, _):
         locals_ = [local_scr[i * group + j] + dot_turned(region, transfer[i * group + j]) for j in range(group)]

time: 111 us -> 110 us (level)
  the two profiles are of different devices: /device:TPU:2 before, /device:TPU:58 now
where the time goes in v6:
time: 110 us
  Pallas kernels  72 us (65%)
  between operations  13.6 us (12%)
  waiting for transfers between devices  12.6 us (11%)
  starting transfers between devices  9.23 us (8%)
  local copies, waits for them, and re-layouts  1.5 us (1%)
    pallas_call x1, Pallas kernels, near_field(): pl.pallas_call(functools.partial(near_kernel, stop=stop, leaf_size=leaf_s...  40.4 us
    pallas_call x1, Pallas kernels, last_field(): pl.pallas_call(functools.partial(last_kernel, begin=begin, leaf_size=leaf...  24.2 us
    pallas_call x1, Pallas kernels, coefficients(): pl.pallas_call(functools.partial(coef_kernel, group=group), grid_spec=plt...  7.42 us
    ppermute x3, waiting for transfers between devices, from_partner(): return lax.ppermute(x, 'leaf', [(i, i ^ distance) for i in range(count)])  6.76 us
    ppermute x1, waiting for transfers between devices, neighbours(): after = lax.ppermute(head, axes, [(i + 1, i) for i in range(count - 1)])  5.6 us
    ppermute x1, starting transfers between devices, neighbours(): before = lax.ppermute(tail, axes, [(i, i + 1) for i in range(count - 1)])  3.48 us
    ppermute x3, starting transfers between devices, from_partner(): return lax.ppermute(x, 'leaf', [(i, i ^ distance) for i in range(count)])  3.38 us
    ppermute x1, starting transfers between devices, neighbours(): after = lax.ppermute(head, axes, [(i + 1, i) for i in range(count - 1)])  2.36 us
  transfers between devices with their start and end apart: 6, of which 5 were waited for; matrix products, arithmetic and copies ran while one was open for 0% of the time, Pallas kernels for 37%

profile of v6, /device:TPU:58, one launch (start us, length us, event | category | flops | bytes accessed | tf_op | source)
XLA Modules:
  0.0 109.9 jit_solution(6878553346866084314)
XLA Ops:
  6.5 0.0 all-gather.3.cloned.1.call-start
  6.5 0.0 copy-start.5
  6.5 0.0 copy-start
  6.5 0.0 copy-start.6
  6.5 7.4 %shard_map.100 = f32[43,8,128]{2,1,0:T(8,128)} custom-call(s32[1]{0:T(128)} %bitcast.2.place_ref.refs_9_, f32[8,20480]{1,0:T(8,128)} %refs_3_.3, f32[40,512,128]{2,1,0:T(8,128)} %refs_18_.1, f32[40,128,128]{2,1,0:T(8,128)} %refs_17_.1, f32[12,128,128]{2,1,0:T(8,128)} %refs_19_.1, f32[12,128,128]{2,1,0:T(8,128)} %refs_19_.1), custom_call_target="tpu_custom_call" | custom-call | flops 209715200 | bytes 13107200 | tf_op jit(solution)/shard_map/pallas_call | solution.py:102
  14.0 0.0 all-gather.3.cloned.1.call-update
  14.0 0.0 copy-done.5
  14.0 0.0 copy-done
  14.1 3.5 %collective-permute-start = (f32[11,1024]{1,0:T(8,128)S(1)}, f32[11,1024]{1,0:T(8,128)S(1)}, u32[]{:S(2)}, u32[]{:S(2)}) collective-permute-start(f32[11,1024]{1,0:T(8,128)S(1)} %pad_maximum_fusion), channel_id=1, source_target_pairs={{0,1},{1,2},{2,3},{3,4},{4,5},{5,6},{6,7},{7,8},{8,9},{9,10},{10,1... | collective-permute-start | bytes 135176 | tf_op jit(solution)/shard_map/ppermute | solution.py:373
  17.6 2.4 %collective-permute-start.1 = (f32[11,1024]{1,0:T(8,128)S(1)}, f32[11,1024]{1,0:T(8,128)S(1)}, u32[]{:S(2)}, u32[]{:S(2)}) collective-permute-start(f32[11,1024]{1,0:T(8,128)S(1)} %pad_maximum_fusion.1), channel_id=1, source_target_pairs={{1,0},{2,1},{3,2},{4,3},{5,4},{6,5},{7,6},{8,7},{9,8},{10,9},{11,1... | collective-permute-start | bytes 135176 | tf_op jit(solution)/shard_map/ppermute | solution.py:374
  20.0 0.3 collective-permute-done
  20.2 0.0 copy-start.3
  20.2 0.0 copy-start.1
  20.3 5.6 %collective-permute-done.1 = f32[11,1024]{1,0:T(8,128)S(1)} collective-permute-done((f32[11,1024]{1,0:T(8,128)S(1)}, f32[11,1024]{1,0:T(8,128)S(1)}, u32[]{:S(2)}, u32[]{:S(2)}) %collective-permute-start.1) | collective-permute-done | bytes 45088 | tf_op jit(solution)/shard_map/ppermute | solution.py:374
  25.9 0.0 copy-start.4
  25.9 0.0 copy-start.2
  25.9 0.0 copy-done.6
  25.9 40.4 %shard_map.101.refs_8_ = f32[8,20480]{1,0:T(8,128)S(1)} custom-call(s32[1]{0:T(128)} %bitcast.refs_0_, s32[2,40]{1,0:T(2,128)S(1)} %bitcast.12, f32[3,20480]{1,0:T(4,128)S(1)} %copy-done.5, f32[8,20480]{1,0:T(8,128)S(1)} %copy-done, f32[3,1024]{1,0:T(4,128)S(1)} %slice.36.refs_4_, f32[8,1024]{1,0:T(8,128)S(1)} %slice.37.refs_5_, ...), custom_call_target="tpu_custom_call" | custom-call | flops 10737418240 | bytes 1802240 | tf_op jit(solution)/shard_map/pallas_call | solution.py:286
  66.2 0.0 copy-done.3
  66.3 0.0 copy-done.1
  66.3 0.0 copy-done.4
  66.3 0.0 copy-done.2
  66.3 0.0 copy-start.7
  66.3 0.8 copy-done.7
  67.1 0.0 all-gather.3.cloned.1.call-done
  67.1 1.0 slice_reduce_fusion
  68.1 0.1 collective-permute-start.2
  68.2 1.2 %collective-permute-done.2.refs_12_ = f32[3,8,128]{2,1,0:T(8,128)S(1)} collective-permute-done((f32[3,8,128]{2,1,0:T(8,128)S(1)}, f32[3,8,128]{2,1,0:T(8,128)S(1)}, u32[]{:S(2)}, u32[]{:S(2)}) %collective-permute-start.2) | collective-permute-done | bytes 12320 | tf_op jit(solution)/shard_map/ppermute | solution.py:382
  69.3 0.0 copy-start.8
  69.4 0.9 collective-permute-start.3
  70.3 2.8 %collective-permute-done.3.refs_13_ = f32[3,8,128]{2,1,0:T(8,128)S(1)} collective-permute-done((f32[3,8,128]{2,1,0:T(8,128)S(1)}, f32[3,8,128]{2,1,0:T(8,128)S(1)}, u32[]{:S(2)}, u32[]{:S(2)}) %collective-permute-start.3) | collective-permute-done | bytes 12320 | tf_op jit(solution)/shard_map/ppermute | solution.py:382
  73.0 0.0 copy-start.9
  73.1 2.4 %collective-permute-start.4 = (f32[3,8,128]{2,1,0:T(8,128)S(1)}, f32[3,8,128]{2,1,0:T(8,128)S(1)}, u32[]{:S(2)}, u32[]{:S(2)}) collective-permute-start(f32[3,8,128]{2,1,0:T(8,128)S(1)} %add.12), channel_id=1, source_target_pairs={{0,64},{16,80},{32,96},{48,112},{64,0},{80,16},{96,32},{112,48},{1... | collective-permute-start | bytes 36872 | tf_op jit(solution)/shard_map/ppermute | solution.py:382
  75.4 2.8 %collective-permute-done.4.refs_14_ = f32[3,8,128]{2,1,0:T(8,128)S(1)} collective-permute-done((f32[3,8,128]{2,1,0:T(8,128)S(1)}, f32[3,8,128]{2,1,0:T(8,128)S(1)}, u32[]{:S(2)}, u32[]{:S(2)}) %collective-permute-start.4) | collective-permute-done | bytes 12320 | tf_op jit(solution)/shard_map/ppermute | solution.py:382
  78.3 0.0 copy-start.10
  78.3 0.0 copy-done.8
  78.3 0.0 copy-done.9
  78.3 0.6 copy-done.10
  78.9 24.2 %shard_map.102 = f32[8,20480]{1,0:T(8,128)} custom-call(s32[1]{0:T(128)} %bitcast.refs_0_, s32[2,40]{1,0:T(2,128)} %bitcast.11, f32[3,20480]{1,0:T(4,128)} %refs_2_.3, f32[8,20480]{1,0:T(8,128)} %refs_3_.3, f32[3,1024]{1,0:T(4,128)} %copy-done.3, f32[8,1024]{1,0:T(8,128)} %copy-done.1, f32[3,1024]{1,0:T(4,128)} %copy-done.4, f32[8,1024]{1,0:T(8,128)} %copy-done.2, ...), custom_call_target="tpu_custom_call" | custom-call | flops 5368709120 | bytes 1802240 | tf_op jit(solution)/shard_map/pallas_call | solution.py:356
  (10 shorter events, 0.1 us)
Async XLA Ops:
  6.5 60.6 %all-gather.3.cloned.1.call-start = ((), (), s32[]{:S(2)}) async-start(), calls=%async_computation | async-start | bytes 2994176 | tf_op jit(solution)/shard_map/all_gather | solution.py:408
  6.5 7.5 %copy-start.5 = (f32[3,20480]{1,0:T(4,128)S(1)}, f32[3,20480]{1,0:T(4,128)}, u32[]{:S(2)}) copy-start(f32[3,20480]{1,0:T(4,128)} %refs_2_.3) | copy-start | bytes 737284
  6.5 7.5 %copy-start = (f32[8,20480]{1,0:T(8,128)S(1)}, f32[8,20480]{1,0:T(8,128)}, u32[]{:S(2)}) copy-start(f32[8,20480]{1,0:T(8,128)} %refs_3_.3) | copy-start | bytes 1966084
  6.5 19.3 %copy-start.6 = (s32[40,2]{0,1:T(2,128)S(1)}, s32[40,2]{0,1:T(2,128)}, u32[]{:S(2)}) copy-start(s32[40,2]{0,1:T(2,128)} %param.12) | copy-start | bytes 964
  14.1 6.2 %collective-permute-start = (f32[11,1024]{1,0:T(8,128)S(1)}, f32[11,1024]{1,0:T(8,128)S(1)}, u32[]{:S(2)}, u32[]{:S(2)}) collective-permute-start(f32[11,1024]{1,0:T(8,128)S(1)} %pad_maximum_fusion), channel_id=1, source_target_pairs={{0,1},{1,2},{2,3},{3,4},{4,5},{5,6},{6,7},{7,8},{8,9},{9,10},{10,1... | collective-permute-start | bytes 135176 | tf_op jit(solution)/shard_map/ppermute | solution.py:373
  17.6 8.3 %collective-permute-start.1 = (f32[11,1024]{1,0:T(8,128)S(1)}, f32[11,1024]{1,0:T(8,128)S(1)}, u32[]{:S(2)}, u32[]{:S(2)}) collective-permute-start(f32[11,1024]{1,0:T(8,128)S(1)} %pad_maximum_fusion.1), channel_id=1, source_target_pairs={{1,0},{2,1},{3,2},{4,3},{5,4},{6,5},{7,6},{8,7},{9,8},{10,9},{11,1... | collective-permute-start | bytes 135176 | tf_op jit(solution)/shard_map/ppermute | solution.py:374
  20.2 46.0 %copy-start.3 = (f32[3,1024]{1,0:T(4,128)}, f32[3,1024]{1,0:T(4,128)S(1)}, u32[]{:S(2)}) copy-start(f32[3,1024]{1,0:T(4,128)S(1)} %slice.36.refs_4_) | copy-start | bytes 36868
  20.2 46.0 %copy-start.1 = (f32[8,1024]{1,0:T(8,128)}, f32[8,1024]{1,0:T(8,128)S(1)}, u32[]{:S(2)}) copy-start(f32[8,1024]{1,0:T(8,128)S(1)} %slice.37.refs_5_) | copy-start | bytes 98308
  25.9 40.4 %copy-start.4 = (f32[3,1024]{1,0:T(4,128)}, f32[3,1024]{1,0:T(4,128)S(1)}, u32[]{:S(2)}) copy-start(f32[3,1024]{1,0:T(4,128)S(1)} %slice.38.refs_6_) | copy-start | bytes 36868
  25.9 40.4 %copy-start.2 = (f32[8,1024]{1,0:T(8,128)}, f32[8,1024]{1,0:T(8,128)S(1)}, u32[]{:S(2)}) copy-start(f32[8,1024]{1,0:T(8,128)S(1)} %slice.39.refs_7_) | copy-start | bytes 98308
  66.3 0.8 copy-start.7
  68.1 1.3 %collective-permute-start.2 = (f32[3,8,128]{2,1,0:T(8,128)S(1)}, f32[3,8,128]{2,1,0:T(8,128)S(1)}, u32[]{:S(2)}, u32[]{:S(2)}) collective-permute-start(f32[3,8,128]{2,1,0:T(8,128)S(1)} %slice_reduce_fusion), channel_id=1, source_target_pairs={{0,16},{16,0},{32,48},{48,32},{64,80},{80,64},{96,112},{112,96},{1... | collective-permute-start | bytes 36872 | tf_op jit(solution)/shard_map/ppermute | solution.py:382
  69.3 8.9 %copy-start.8 = (f32[3,8,128]{2,1,0:T(8,128)}, f32[3,8,128]{2,1,0:T(8,128)S(1)}, u32[]{:S(2)}) copy-start(f32[3,8,128]{2,1,0:T(8,128)S(1)} %collective-permute-done.2.refs_12_) | copy-start | bytes 36868
  69.4 3.7 %collective-permute-start.3 = (f32[3,8,128]{2,1,0:T(8,128)S(1)}, f32[3,8,128]{2,1,0:T(8,128)S(1)}, u32[]{:S(2)}, u32[]{:S(2)}) collective-permute-start(f32[3,8,128]{2,1,0:T(8,128)S(1)} %add.11), channel_id=1, source_target_pairs={{0,32},{16,48},{32,0},{48,16},{64,96},{80,112},{96,64},{112,80},{1... | collective-permute-start | bytes 36872 | tf_op jit(solution)/shard_map/ppermute | solution.py:382
  73.0 5.2 %copy-start.9 = (f32[3,8,128]{2,1,0:T(8,128)}, f32[3,8,128]{2,1,0:T(8,128)S(1)}, u32[]{:S(2)}) copy-start(f32[3,8,128]{2,1,0:T(8,128)S(1)} %collective-permute-done.3.refs_13_) | copy-start | bytes 36868
  73.1 5.2 %collective-permute-start.4 = (f32[3,8,128]{2,1,0:T(8,128)S(1)}, f32[3,8,128]{2,1,0:T(8,128)S(1)}, u32[]{:S(2)}, u32[]{:S(2)}) collective-permute-start(f32[3,8,128]{2,1,0:T(8,128)S(1)} %add.12), channel_id=1, source_target_pairs={{0,64},{16,80},{32,96},{48,112},{64,0},{80,16},{96,32},{112,48},{1... | collective-permute-start | bytes 36872 | tf_op jit(solution)/shard_map/ppermute | solution.py:382
  78.3 0.6 copy-start.10
Sparse Core Ops, SparseCore 0:
  14.1 46.9 all-gather.2

commit v7 on v6

--- a/solution.py
+++ b/solution.py
@@ -332,7 +332,7 @@
             local_scr[target_ref[k, p]] += products[k]
         return 0
 
-    lax.fori_loop(0, peers, far, 0, unroll=2)
+    lax.fori_loop(0, peers, far, 0, unroll=4)
 
     group = 8
 

time: 110 us -> 109 us (level)
  the two profiles are of different devices: /device:TPU:58 before, /device:TPU:30 now
where the time goes in v7:
time: 109 us; the launch traced here: 108 us
  Pallas kernels  69.6 us (64%)
  between operations  13.6 us (12%)
  waiting for transfers between devices  13.3 us (12%)
  starting transfers between devices  8.55 us (8%)
  local copies, waits for them, and re-layouts  1.5 us (1%)
    pallas_call x1, Pallas kernels, near_field(): pl.pallas_call(functools.partial(near_kernel, stop=stop, leaf_size=leaf_s...  40.5 us
    pallas_call x1, Pallas kernels, last_field(): pl.pallas_call(functools.partial(last_kernel, begin=begin, leaf_size=leaf...  21.7 us
    ppermute x3, waiting for transfers between devices, from_partner(): return lax.ppermute(x, 'leaf', [(i, i ^ distance) for i in range(count)])  7.44 us
    pallas_call x1, Pallas kernels, coefficients(): pl.pallas_call(functools.partial(coef_kernel, group=group), grid_spec=plt...  7.42 us
    ppermute x1, waiting for transfers between devices, neighbours(): after = lax.ppermute(head, axes, [(i + 1, i) for i in range(count - 1)])  5.6 us
    ppermute x1, starting transfers between devices, neighbours(): before = lax.ppermute(tail, axes, [(i, i + 1) for i in range(count - 1)])  3.48 us
    ppermute x3, starting transfers between devices, from_partner(): return lax.ppermute(x, 'leaf', [(i, i ^ distance) for i in range(count)])  2.71 us
    ppermute x1, starting transfers between devices, neighbours(): after = lax.ppermute(head, axes, [(i + 1, i) for i in range(count - 1)])  2.36 us
  transfers between devices with their start and end apart: 6, of which 5 were waited for; matrix products, arithmetic and copies ran while one was open for 0% of the time, Pallas kernels for 38%

profile of v7, /device:TPU:30, one launch (start us, length us, event | category | flops | bytes accessed | tf_op | source)
XLA Modules:
  0.0 107.6 jit_solution(1280946501598254262)
XLA Ops:
  6.5 0.0 all-gather.3.cloned.1.call-start
  6.5 0.0 copy-start.5
  6.5 0.0 copy-start
  6.5 0.0 copy-start.6
  6.5 7.4 %shard_map.100 = f32[43,8,128]{2,1,0:T(8,128)} custom-call(s32[1]{0:T(128)} %bitcast.2.place_ref.refs_9_, f32[8,20480]{1,0:T(8,128)} %refs_3_.3, f32[40,512,128]{2,1,0:T(8,128)} %refs_18_.1, f32[40,128,128]{2,1,0:T(8,128)} %refs_17_.1, f32[12,128,128]{2,1,0:T(8,128)} %refs_19_.1, f32[12,128,128]{2,1,0:T(8,128)} %refs_19_.1), custom_call_target="tpu_custom_call" | custom-call | flops 209715200 | bytes 13107200 | tf_op jit(solution)/shard_map/pallas_call | solution.py:102
  14.0 0.0 all-gather.3.cloned.1.call-update
  14.0 0.0 copy-done.5
  14.0 0.0 copy-done
  14.1 3.5 %collective-permute-start = (f32[11,1024]{1,0:T(8,128)S(1)}, f32[11,1024]{1,0:T(8,128)S(1)}, u32[]{:S(2)}, u32[]{:S(2)}) collective-permute-start(f32[11,1024]{1,0:T(8,128)S(1)} %pad_maximum_fusion), channel_id=1, source_target_pairs={{0,1},{1,2},{2,3},{3,4},{4,5},{5,6},{6,7},{7,8},{8,9},{9,10},{10,1... | collective-permute-start | bytes 135176 | tf_op jit(solution)/shard_map/ppermute | solution.py:373
  17.6 2.4 %collective-permute-start.1 = (f32[11,1024]{1,0:T(8,128)S(1)}, f32[11,1024]{1,0:T(8,128)S(1)}, u32[]{:S(2)}, u32[]{:S(2)}) collective-permute-start(f32[11,1024]{1,0:T(8,128)S(1)} %pad_maximum_fusion.1), channel_id=1, source_target_pairs={{1,0},{2,1},{3,2},{4,3},{5,4},{6,5},{7,6},{8,7},{9,8},{10,9},{11,1... | collective-permute-start | bytes 135176 | tf_op jit(solution)/shard_map/ppermute | solution.py:374
  20.0 0.3 collective-permute-done
  20.2 0.0 copy-start.3
  20.2 0.0 copy-start.1
  20.3 5.6 %collective-permute-done.1 = f32[11,1024]{1,0:T(8,128)S(1)} collective-permute-done((f32[11,1024]{1,0:T(8,128)S(1)}, f32[11,1024]{1,0:T(8,128)S(1)}, u32[]{:S(2)}, u32[]{:S(2)}) %collective-permute-start.1) | collective-permute-done | bytes 45088 | tf_op jit(solution)/shard_map/ppermute | solution.py:374
  25.9 0.0 copy-start.4
  25.9 0.0 copy-start.2
  25.9 0.0 copy-done.6
  25.9 40.5 %shard_map.101.refs_8_ = f32[8,20480]{1,0:T(8,128)S(1)} custom-call(s32[1]{0:T(128)} %bitcast.refs_0_, s32[2,40]{1,0:T(2,128)S(1)} %bitcast.12, f32[3,20480]{1,0:T(4,128)S(1)} %copy-done.5, f32[8,20480]{1,0:T(8,128)S(1)} %copy-done, f32[3,1024]{1,0:T(4,128)S(1)} %slice.36.refs_4_, f32[8,1024]{1,0:T(8,128)S(1)} %slice.37.refs_5_, ...), custom_call_target="tpu_custom_call" | custom-call | flops 10737418240 | bytes 1802240 | tf_op jit(solution)/shard_map/pallas_call | solution.py:286
  66.4 0.0 copy-done.3
  66.4 0.0 copy-done.1
  66.4 0.0 copy-done.4
  66.4 0.0 copy-done.2
  66.4 0.0 copy-start.7
  66.4 0.8 copy-done.7
  67.3 0.0 all-gather.3.cloned.1.call-done
  67.3 1.0 slice_reduce_fusion
  68.2 0.1 collective-permute-start.2
  68.3 1.2 %collective-permute-done.2.refs_12_ = f32[3,8,128]{2,1,0:T(8,128)S(1)} collective-permute-done((f32[3,8,128]{2,1,0:T(8,128)S(1)}, f32[3,8,128]{2,1,0:T(8,128)S(1)}, u32[]{:S(2)}, u32[]{:S(2)}) %collective-permute-start.2) | collective-permute-done | bytes 12320 | tf_op jit(solution)/shard_map/ppermute | solution.py:382
  69.5 0.0 copy-start.8
  69.5 1.0 collective-permute-start.3
  70.4 2.7 %collective-permute-done.3.refs_13_ = f32[3,8,128]{2,1,0:T(8,128)S(1)} collective-permute-done((f32[3,8,128]{2,1,0:T(8,128)S(1)}, f32[3,8,128]{2,1,0:T(8,128)S(1)}, u32[]{:S(2)}, u32[]{:S(2)}) %collective-permute-start.3) | collective-permute-done | bytes 12320 | tf_op jit(solution)/shard_map/ppermute | solution.py:382
  73.2 0.0 copy-start.9
  73.2 1.7 %collective-permute-start.4 = (f32[3,8,128]{2,1,0:T(8,128)S(1)}, f32[3,8,128]{2,1,0:T(8,128)S(1)}, u32[]{:S(2)}, u32[]{:S(2)}) collective-permute-start(f32[3,8,128]{2,1,0:T(8,128)S(1)} %add.12), channel_id=1, source_target_pairs={{0,64},{16,80},{32,96},{48,112},{64,0},{80,16},{96,32},{112,48},{1... | collective-permute-start | bytes 36872 | tf_op jit(solution)/shard_map/ppermute | solution.py:382
  74.8 3.5 %collective-permute-done.4.refs_14_ = f32[3,8,128]{2,1,0:T(8,128)S(1)} collective-permute-done((f32[3,8,128]{2,1,0:T(8,128)S(1)}, f32[3,8,128]{2,1,0:T(8,128)S(1)}, u32[]{:S(2)}, u32[]{:S(2)}) %collective-permute-start.4) | collective-permute-done | bytes 12320 | tf_op jit(solution)/shard_map/ppermute | solution.py:382
  78.4 0.0 copy-start.10
  78.4 0.0 copy-done.8
  78.4 0.0 copy-done.9
  78.4 0.6 copy-done.10
  79.0 21.7 %shard_map.102 = f32[8,20480]{1,0:T(8,128)} custom-call(s32[1]{0:T(128)} %bitcast.refs_0_, s32[2,40]{1,0:T(2,128)} %bitcast.11, f32[3,20480]{1,0:T(4,128)} %refs_2_.3, f32[8,20480]{1,0:T(8,128)} %refs_3_.3, f32[3,1024]{1,0:T(4,128)} %copy-done.3, f32[8,1024]{1,0:T(8,128)} %copy-done.1, f32[3,1024]{1,0:T(4,128)} %copy-done.4, f32[8,1024]{1,0:T(8,128)} %copy-done.2, ...), custom_call_target="tpu_custom_call" | custom-call | flops 5368709120 | bytes 1802240 | tf_op jit(solution)/shard_map/pallas_call | solution.py:356
  (10 shorter events, 0.1 us)
Async XLA Ops:
  6.5 60.7 %all-gather.3.cloned.1.call-start = ((), (), s32[]{:S(2)}) async-start(), calls=%async_computation | async-start | bytes 2994176 | tf_op jit(solution)/shard_map/all_gather | solution.py:408
  6.5 7.5 %copy-start.5 = (f32[3,20480]{1,0:T(4,128)S(1)}, f32[3,20480]{1,0:T(4,128)}, u32[]{:S(2)}) copy-start(f32[3,20480]{1,0:T(4,128)} %refs_2_.3) | copy-start | bytes 737284
  6.5 7.5 %copy-start = (f32[8,20480]{1,0:T(8,128)S(1)}, f32[8,20480]{1,0:T(8,128)}, u32[]{:S(2)}) copy-start(f32[8,20480]{1,0:T(8,128)} %refs_3_.3) | copy-start | bytes 1966084
  6.5 19.3 %copy-start.6 = (s32[40,2]{0,1:T(2,128)S(1)}, s32[40,2]{0,1:T(2,128)}, u32[]{:S(2)}) copy-start(s32[40,2]{0,1:T(2,128)} %param.12) | copy-start | bytes 964
  14.1 6.2 %collective-permute-start = (f32[11,1024]{1,0:T(8,128)S(1)}, f32[11,1024]{1,0:T(8,128)S(1)}, u32[]{:S(2)}, u32[]{:S(2)}) collective-permute-start(f32[11,1024]{1,0:T(8,128)S(1)} %pad_maximum_fusion), channel_id=1, source_target_pairs={{0,1},{1,2},{2,3},{3,4},{4,5},{5,6},{6,7},{7,8},{8,9},{9,10},{10,1... | collective-permute-start | bytes 135176 | tf_op jit(solution)/shard_map/ppermute | solution.py:373
  17.6 8.3 %collective-permute-start.1 = (f32[11,1024]{1,0:T(8,128)S(1)}, f32[11,1024]{1,0:T(8,128)S(1)}, u32[]{:S(2)}, u32[]{:S(2)}) collective-permute-start(f32[11,1024]{1,0:T(8,128)S(1)} %pad_maximum_fusion.1), channel_id=1, source_target_pairs={{1,0},{2,1},{3,2},{4,3},{5,4},{6,5},{7,6},{8,7},{9,8},{10,9},{11,1... | collective-permute-start | bytes 135176 | tf_op jit(solution)/shard_map/ppermute | solution.py:374
  20.2 46.1 %copy-start.3 = (f32[3,1024]{1,0:T(4,128)}, f32[3,1024]{1,0:T(4,128)S(1)}, u32[]{:S(2)}) copy-start(f32[3,1024]{1,0:T(4,128)S(1)} %slice.36.refs_4_) | copy-start | bytes 36868
  20.2 46.1 %copy-start.1 = (f32[8,1024]{1,0:T(8,128)}, f32[8,1024]{1,0:T(8,128)S(1)}, u32[]{:S(2)}) copy-start(f32[8,1024]{1,0:T(8,128)S(1)} %slice.37.refs_5_) | copy-start | bytes 98308
  25.9 40.5 %copy-start.4 = (f32[3,1024]{1,0:T(4,128)}, f32[3,1024]{1,0:T(4,128)S(1)}, u32[]{:S(2)}) copy-start(f32[3,1024]{1,0:T(4,128)S(1)} %slice.38.refs_6_) | copy-start | bytes 36868
  25.9 40.5 %copy-start.2 = (f32[8,1024]{1,0:T(8,128)}, f32[8,1024]{1,0:T(8,128)S(1)}, u32[]{:S(2)}) copy-start(f32[8,1024]{1,0:T(8,128)S(1)} %slice.39.refs_7_) | copy-start | bytes 98308
  66.4 0.8 copy-start.7
  68.2 1.3 %collective-permute-start.2 = (f32[3,8,128]{2,1,0:T(8,128)S(1)}, f32[3,8,128]{2,1,0:T(8,128)S(1)}, u32[]{:S(2)}, u32[]{:S(2)}) collective-permute-start(f32[3,8,128]{2,1,0:T(8,128)S(1)} %slice_reduce_fusion), channel_id=1, source_target_pairs={{0,16},{16,0},{32,48},{48,32},{64,80},{80,64},{96,112},{112,96},{1... | collective-permute-start | bytes 36872 | tf_op jit(solution)/shard_map/ppermute | solution.py:382
  69.5 8.9 %copy-start.8 = (f32[3,8,128]{2,1,0:T(8,128)}, f32[3,8,128]{2,1,0:T(8,128)S(1)}, u32[]{:S(2)}) copy-start(f32[3,8,128]{2,1,0:T(8,128)S(1)} %collective-permute-done.2.refs_12_) | copy-start | bytes 36868
  69.5 3.7 %collective-permute-start.3 = (f32[3,8,128]{2,1,0:T(8,128)S(1)}, f32[3,8,128]{2,1,0:T(8,128)S(1)}, u32[]{:S(2)}, u32[]{:S(2)}) collective-permute-start(f32[3,8,128]{2,1,0:T(8,128)S(1)} %add.11), channel_id=1, source_target_pairs={{0,32},{16,48},{32,0},{48,16},{64,96},{80,112},{96,64},{112,80},{1... | collective-permute-start | bytes 36872 | tf_op jit(solution)/shard_map/ppermute | solution.py:382
  73.2 5.2 %copy-start.9 = (f32[3,8,128]{2,1,0:T(8,128)}, f32[3,8,128]{2,1,0:T(8,128)S(1)}, u32[]{:S(2)}) copy-start(f32[3,8,128]{2,1,0:T(8,128)S(1)} %collective-permute-done.3.refs_13_) | copy-start | bytes 36868
  73.2 5.2 %collective-permute-start.4 = (f32[3,8,128]{2,1,0:T(8,128)S(1)}, f32[3,8,128]{2,1,0:T(8,128)S(1)}, u32[]{:S(2)}, u32[]{:S(2)}) collective-permute-start(f32[3,8,128]{2,1,0:T(8,128)S(1)} %add.12), channel_id=1, source_target_pairs={{0,64},{16,80},{32,96},{48,112},{64,0},{80,16},{96,32},{112,48},{1... | collective-permute-start | bytes 36872 | tf_op jit(solution)/shard_map/ppermute | solution.py:382
  78.4 0.6 copy-start.10
Sparse Core Ops, SparseCore 0:
  14.1 48.6 all-gather.2
